TPU v7x, 32 devices: a whole 2x2x4 slice. The times are simulated.
32 devices in a mesh: dom: 8 (over z, core), sub: 4 (over y, x).
Axes of the slice: x: 2, y: 2, z: 4, core: 2. Of those that a mesh axis runs over, the one named last changes fastest.
Arguments:
- modal_state: float32 [56, 9, 4096], P(None, None, ('dom', 'sub')), may hold values from -6 to 6
- stiffness: float32 [3, 56, 56], replicated, may hold values from -0.75 to 0.75
- jacobians: float32 [3, 9, 9, 4096], P(None, None, None, ('dom', 'sub')), may hold values from -1.25 to 1.25
- flux_solvers: float32 [2, 4, 9, 9, 4096], P(None, None, None, None, ('dom', 'sub')), may hold values from -0.75 to 0.75
- projector: float32 [4, 21, 56], replicated, may hold values from -0.75 to 0.75
- rotations: float32 [3, 21, 21], replicated, may hold values from -1.25 to 1.25
- yield_stress: float32 [4096], P(('dom', 'sub')), may hold values from 0.5 to 8
- cluster: int32 [4096], P(('dom', 'sub')), may hold values from 0 to 1
- orient: int32 [4, 4096], P(None, ('dom', 'sub')), may hold values from 0 to 2
- neighbour_slot: int32 [4, 4096], P(None, ('dom', 'sub')), may hold values from 0 to 703, as said below
- send_map: int32 [6144], P(('dom', 'sub')), may hold values from 0 to 511, as said below
Outputs:
- updated: float32 [56, 9, 4096], P(None, None, ('dom', 'sub'))
Inputs may be any that keep to these rules, and one draw needn't show every extreme that they name: `neighbour_slot`: within one partition every received slot 512 + r is named by exactly one face; the other faces name local faces. `send_map`: the 192 entries of one partition are distinct local face numbers.
All inputs are finite; a program needn't handle non-finite values.
Results may differ from a plain program's by a relative error of at most 0.0003.
Values sent between devices are 32-bit elements; how exact they have to be, the bound alone decides.
No kernel may reach another device: no remote copies, remote signals or barrier semaphores. Data moves between devices by JAX's collectives and lax.ppermute only.
A program may use at most 64 MiB of HBM per device.

v0:
```python
import jax
import jax.numpy as jnp
from jax import lax
from jax.experimental import pallas as pl
from jax.experimental.pallas import tpu as pltpu
from jax.sharding import PartitionSpec as P

ORDER = 6
SLOTS_DOM = 64
SLOTS_SUB = 32
ROWS = 24
GROUP = 3

F32 = jnp.float32
BF16 = jnp.bfloat16
EXACT = lax.Precision.HIGHEST

DOM_GROUPS = ((0, 5), (5, 4))
SUB_GROUPS = ((0, 3), (3, 2), (5, 2), (7, 2))


def iota(shape, dim):
    return lax.broadcasted_iota(jnp.int32, shape, dim)


def dot(a, b):
    return jnp.dot(a, b, preferred_element_type=F32)


def exact_dot(a, b):
    return jnp.dot(a, b, precision=EXACT, preferred_element_type=F32)


def halves(value):
    high = value.astype(BF16)
    return high, (value - high.astype(F32)).astype(BF16)


def one_hot(index_row, first, count, modulus=None):
    number = iota((count, index_row.shape[1]), 0)
    if modulus is not None:
        number = lax.rem(number, modulus)
    return jnp.where(number + first == index_row, 1.0, 0.0).astype(BF16)


def fold_depth(basis):
    return -(-3 * basis // 64) * 64


def fold_rows(value):
    basis, lanes = value.shape
    high = value.astype(BF16).astype(F32)
    rest = jnp.zeros((fold_depth(basis) - 3 * basis, lanes), F32)
    return jnp.concatenate([high, high, value - high, rest], axis=0).astype(BF16)


def fold_columns(matrix):
    basis = matrix.shape[1]
    depth = fold_depth(basis)
    high, low = halves(matrix)
    row, column = iota((basis, depth), 0), iota((basis, depth), 1)
    outer = jnp.where((column == row) | (column == row + 2 * basis), 1.0, 0.0).astype(BF16)
    inner = jnp.where(column == row + basis, 1.0, 0.0).astype(BF16)
    return (dot(high, outer) + dot(low, inner)).astype(BF16)


def mix_jacobians(stiffened, jac, basis, quants, lanes, write):
    for start in range(0, quants, GROUP):
        totals = [None] * GROUP
        for q in range(quants):
            for d in range(3):
                block = stiffened[d * basis:(d + 1) * basis, q * lanes:(q + 1) * lanes]
                for i in range(GROUP):
                    term = block * jac[q, start + i, d:d + 1, :]
                    totals[i] = term if totals[i] is None else totals[i] + term
        for i in range(GROUP):
            write(start + i, totals[i])


def mix_faces(table, flux, side, quants, lanes, write):
    for f in range(4):
        blocks = [
            table[q * ROWS:(q + 1) * ROWS, f * lanes:(f + 1) * lanes] for q in range(quants)
        ]
        for p in range(quants):
            total = blocks[0] * flux[side, 0, p, f:f + 1, :]
            for q in range(1, quants):
                total = total + blocks[q] * flux[side, q, p, f:f + 1, :]
            write(f, p, total)


def fill_projector(projector, padded):
    modes, faces, basis = projector.shape
    padded[...] = jnp.zeros(padded.shape, F32)
    for f in range(faces):
        for m in range(modes):
            padded[f * ROWS + m:f * ROWS + m + 1, 0:basis] = projector[m, f:f + 1, :]


def predict(stiff_fold, jac, folded, stiffened, first, second, basis, quants, lanes):
    def step(_, scales):
        factor, power, number = scales
        stiffened[...] = dot(stiff_fold, folded[...])

        def write(p, total):
            folded[:, p * lanes:(p + 1) * lanes] = fold_rows(total)
            first[p] = first[p] + factor * total
            if second is not None:
                second[p] = second[p] + (factor * (power - 1.0)) * total

        mix_jacobians(stiffened, jac, basis, quants, lanes, write)
        return factor / (number + 1.0), power * 2.0, number + 1.0

    lax.fori_loop(0, ORDER - 1, step, (jnp.float32(0.5), jnp.float32(4.0), jnp.float32(2.0)))


def project_table(padded, folded, table, basis, quants, lanes):
    flat = dot(fold_columns(padded[:, 0:basis]), folded[...])
    for q in range(quants):
        for f in range(4):
            table[q * ROWS:(q + 1) * ROWS, f * lanes:(f + 1) * lanes] = flat[
                f * ROWS:(f + 1) * ROWS, q * lanes:(q + 1) * lanes
            ]


def pick_sends(table, send_row, outs, lanes):
    faces = table.shape[1]
    low = jnp.broadcast_to(send_row[:, 0:lanes], (8, lanes))
    lane = iota((8, lanes), 1)
    turned = pltpu.roll(low, SLOTS_DOM, 1)
    high = jnp.broadcast_to(send_row[:, lanes:2 * lanes], (8, lanes))
    pieces = [
        jnp.where(lane < SLOTS_DOM, low, turned),
        jnp.where(lane < SLOTS_DOM, turned, low),
    ]
    spread = jnp.where(lane < 2 * SLOTS_SUB, high, pltpu.roll(high, 2 * SLOTS_SUB, 1))
    moved = pltpu.roll(spread, SLOTS_SUB, 1)
    even = lax.rem(lane, 2 * SLOTS_SUB) < SLOTS_SUB
    pieces += [jnp.where(even, spread, moved), jnp.where(even, moved, spread)]
    index = jnp.concatenate([piece[0:1] for piece in pieces], axis=1)
    chosen = one_hot(index, 0, faces)
    upper, lower = halves(table[...])
    sent = dot(upper, chosen) + dot(lower, chosen)
    for k, (out, groups) in enumerate(
        zip(outs, (DOM_GROUPS, DOM_GROUPS, SUB_GROUPS, SUB_GROUPS))
    ):
        width = lanes // len(groups)
        values = sent[:, k * lanes:(k + 1) * lanes]
        start, count = groups[0]
        packed = values[0:count * ROWS]
        least = min(count for _, count in groups) * ROWS
        place = iota((least, lanes), 1)
        head = packed[0:least]
        for g, (start, _) in enumerate(groups):
            if g:
                head = jnp.where(
                    place >= g * width, values[start * ROWS:start * ROWS + least], head
                )
        out[0:least] = head
        out[least:count * ROWS] = packed[least:]


def spread_received(arrived, groups, lanes):
    width = lanes // len(groups)
    parts = []
    for g, (_, count) in enumerate(groups):
        place = iota((count * ROWS, lanes), 1)
        mine = (place >= g * width) & (place < (g + 1) * width)
        parts.append(jnp.where(mine, arrived[0:count * ROWS], 0.0))
    return jnp.concatenate(parts, axis=0)


def pick_local(table, slot, faces):
    chosen = jnp.concatenate([one_hot(slot[f:f + 1], 0, faces) for f in range(4)], axis=1)
    upper, lower = halves(table)
    return dot(upper, chosen) + dot(lower, chosen)


def pick_received(arrived, slot, faces, lanes):
    spread = jnp.concatenate(
        [
            spread_received(item[...], groups, lanes)
            for item, groups in zip(arrived, (DOM_GROUPS, DOM_GROUPS, SUB_GROUPS, SUB_GROUPS))
        ],
        axis=1,
    )
    starts = (faces, faces + SLOTS_DOM, faces + 2 * SLOTS_DOM, faces + 2 * SLOTS_DOM + SLOTS_SUB)
    widths = (SLOTS_DOM, SLOTS_DOM, SLOTS_SUB, SLOTS_SUB)
    chosen = jnp.concatenate(
        [
            jnp.concatenate(
                [one_hot(slot[f:f + 1], first, lanes, width) for f in range(4)], axis=1
            )
            for first, width in zip(starts, widths)
        ],
        axis=0,
    )
    upper, lower = halves(spread)
    return dot(upper, chosen) + dot(lower, chosen)


def lift(weights, high, low):
    upper, lower = halves(weights)
    return dot(upper, high) + dot(lower, high) + dot(upper, low)


def local_update(
    base, integral, table, jac, stiffness, flux, lifting, folded, stiffened, solved, write,
    basis, quants, lanes,
):
    for q in range(quants):
        folded[:, q * lanes:(q + 1) * lanes] = fold_rows(integral(q))
    turned = jnp.concatenate([stiffness[d].T for d in range(3)], axis=0)
    stiffened[...] = dot(fold_columns(turned), folded[...])

    def keep(f, p, total):
        solved[f * ROWS:(f + 1) * ROWS, p * lanes:(p + 1) * lanes] = total

    mix_faces(table, flux, 0, quants, lanes, keep)
    high, low = halves(solved[...])
    own = lift(lifting, high, low)
    mix_jacobians(
        stiffened, jac, basis, quants, lanes,
        lambda p, total: write(p, base(p) + total - own[:, p * lanes:(p + 1) * lanes]),
    )


def near_lift(picked, flux, orient, lifting, solved, quants, lanes):
    block = 4 * ROWS

    def keep(f, p, total):
        upper = total.astype(BF16).astype(F32)
        lower = total - upper
        for o in range(3):
            mine = orient[f:f + 1] == o
            row = o * block + f * ROWS
            solved[row:row + ROWS, p * lanes:(p + 1) * lanes] = jnp.where(mine, upper, 0.0)
            row += 3 * block
            solved[row:row + ROWS, p * lanes:(p + 1) * lanes] = jnp.where(mine, lower, 0.0)

    mix_faces(picked, flux, 1, quants, lanes, keep)
    depth = 3 * block
    return lift(lifting, solved[0:depth].astype(BF16), solved[depth:2 * depth].astype(BF16))


def near_lifting(own_lifting, rotations):
    count, modes, _ = rotations.shape
    block = 4 * ROWS
    row, column = iota((modes, count * block), 0), iota((modes, count * block), 1)
    turned = jnp.zeros((modes, count * block), F32)
    for o in range(count):
        spot = (lax.rem(column, ROWS) == row) & (lax.div(column, block) == o)
        turned = turned + exact_dot(rotations[o], jnp.where(spot, 1.0, 0.0))
    row, column = iota((block, modes), 0), iota((block, modes), 1)
    tall = exact_dot(jnp.where(lax.rem(row, ROWS) == column, 1.0, 0.0), turned)
    row, column = iota(tall.shape, 0), iota(tall.shape, 1)
    same = lax.div(row, ROWS) == lax.div(lax.rem(column, block), ROWS)
    return exact_dot(own_lifting, jnp.where(same, tall, 0.0))


def first_kernel(
    state, jac, stiffness, projector, send_row,
    first, second, table, to_lower, to_upper, to_left, to_right,
    folded, stiffened, padded,
):
    quants, basis, lanes = state.shape
    for q in range(quants):
        value = state[q]
        first[q] = value
        second[q] = value
        folded[:, q * lanes:(q + 1) * lanes] = fold_rows(value)
    fill_projector(projector, padded)
    stacked = jnp.concatenate([stiffness[d] for d in range(3)], axis=0)
    predict(
        fold_columns(stacked), jac, folded, stiffened, first, second, basis, quants, lanes
    )
    for q in range(quants):
        folded[:, q * lanes:(q + 1) * lanes] = fold_rows(first[q])
    project_table(padded, folded, table, basis, quants, lanes)
    pick_sends(table, send_row, (to_lower, to_upper, to_left, to_right), lanes)


def second_kernel(
    state, first, table, jac, stiffness, projector, rotations, flux, slot,
    part, picked, lifting,
    folded, stiffened, solved, padded,
):
    quants, basis, lanes = state.shape
    fill_projector(projector, padded)
    own_lifting = padded[...].T[0:basis]
    lifting[...] = near_lifting(own_lifting, rotations)
    picked[...] = pick_local(table[...], slot, 4 * lanes)

    def write(p, value):
        part[p] = value

    local_update(
        lambda p: state[p], lambda q: first[q], table, jac, stiffness, flux, own_lifting,
        folded, stiffened, solved, write, basis, quants, lanes,
    )


def third_kernel(
    state, first, second, part, picked_local, from_lower, from_upper, from_left, from_right,
    jac, stiffness, projector, flux, slot, orient, cluster, lifting, send_row,
    middle, integral, picked, table, to_lower, to_upper, to_left, to_right,
    folded, stiffened, solved, padded,
):
    quants, basis, lanes = state.shape
    fill_projector(projector, padded)
    picked[...] = picked_local[...] + pick_received(
        (from_lower, from_upper, from_left, from_right), slot, 4 * lanes, lanes
    )
    near = near_lift(picked, flux, orient, lifting[...], solved, quants, lanes)
    fine = cluster[...] == 0
    for q in range(quants):
        value = jnp.where(fine, part[q] - near[:, q * lanes:(q + 1) * lanes], state[q])
        middle[q] = value
        integral[q] = value
        folded[:, q * lanes:(q + 1) * lanes] = fold_rows(value)
    stacked = jnp.concatenate([stiffness[d] for d in range(3)], axis=0)
    predict(
        fold_columns(stacked), jac, folded, stiffened, integral, None, basis, quants, lanes
    )
    for q in range(quants):
        fine_first = integral[q]
        late = jnp.where(fine, fine_first, second[q])
        folded[:, q * lanes:(q + 1) * lanes] = fold_rows(late)
        integral[q] = jnp.where(fine, fine_first, first[q] + second[q])
    project_table(padded, folded, table, basis, quants, lanes)
    pick_sends(table, send_row, (to_lower, to_upper, to_left, to_right), lanes)


def fourth_kernel(
    middle, integral, table_one, table_two, picked_one, jac, stiffness, projector, flux, slot,
    cluster,
    part, picked,
    folded, stiffened, solved, padded, total_table,
):
    quants, basis, lanes = middle.shape
    fill_projector(projector, padded)
    own_lifting = padded[...].T[0:basis]
    coarse = jnp.concatenate([cluster[...] != 0] * 4, axis=1)
    total_table[...] = table_two[...] + jnp.where(coarse, table_one[...], 0.0)
    picked[...] = pick_local(table_two[...], slot, 4 * lanes) + jnp.where(
        coarse, picked_one[...], 0.0
    )

    def write(p, value):
        part[p] = value

    local_update(
        lambda p: middle[p], lambda q: integral[q], total_table, jac, stiffness, flux,
        own_lifting, folded, stiffened, solved, write, basis, quants, lanes,
    )


def fifth_kernel(
    part, picked_local, from_lower, from_upper, from_left, from_right, flux, slot, orient,
    lifting, yield_stress,
    updated,
    solved, picked,
):
    quants, basis, lanes = part.shape
    picked[...] = picked_local[...] + pick_received(
        (from_lower, from_upper, from_left, from_right), slot, 4 * lanes, lanes
    )
    near = near_lift(picked, flux, orient, lifting[...], solved, quants, lanes)
    stepped = [part[q] - near[:, q * lanes:(q + 1) * lanes] for q in range(quants)]
    mean_part = (stepped[0] + stepped[1] + stepped[2]) / 3.0
    spread = [stepped[q] - mean_part for q in range(3)]
    normal = [item[0:1] for item in spread]
    shear = [stepped[q][0:1] for q in range(3, 6)]
    second_inv = 0.5 * (normal[0] ** 2 + normal[1] ** 2 + normal[2] ** 2) + (
        shear[0] ** 2 + shear[1] ** 2 + shear[2] ** 2
    )
    limit = yield_stress[...]
    scaling = limit / jnp.maximum(jnp.sqrt(second_inv), limit)
    for q in range(3):
        updated[q] = mean_part + scaling * spread[q]
    for q in range(3, 6):
        updated[q] = scaling * stepped[q]
    for q in range(6, quants):
        updated[q] = stepped[q]


def run(body, outs, scratch, *operands):
    vmem = pl.BlockSpec(memory_space=pltpu.VMEM)
    return pl.pallas_call(
        body,
        out_shape=[jax.ShapeDtypeStruct(shape, F32) for shape in outs],
        in_specs=[vmem] * len(operands),
        out_specs=[vmem] * len(outs),
        scratch_shapes=[pltpu.VMEM(shape, kind) for shape, kind in scratch],
        compiler_params=pltpu.CompilerParams(vmem_limit_bytes=32 * 1024 * 1024),
        name=body.__name__,
    )(*operands)


def exchange(sends):
    to_lower, to_upper, to_left, to_right = sends

    def shift(value, axis, step):
        size = lax.axis_size(axis)
        pairs = [(i, i + step) for i in range(size) if 0 <= i + step < size]
        return lax.ppermute(value, axis, pairs)

    return (
        shift(to_upper, "dom", 1),
        shift(to_lower, "dom", -1),
        shift(to_right, "sub", 1),
        shift(to_left, "sub", -1),
    )


def on_device(
    modal_state,
    stiffness,
    jacobians,
    flux_solvers,
    projector,
    rotations,
    yield_stress,
    cluster,
    orient,
    neighbour_slot,
    send_map,
):
    basis, quants, lanes = modal_state.shape
    state = jnp.transpose(modal_state, (1, 0, 2))
    jac = jnp.transpose(jacobians, (1, 2, 0, 3))
    flux = jnp.transpose(flux_solvers, (0, 2, 3, 1, 4))
    proj = jnp.transpose(projector, (1, 0, 2))
    cluster = cluster.reshape(1, lanes)
    limit = yield_stress.reshape(1, lanes)
    send_row = jnp.pad(send_map, (0, 2 * lanes - send_map.shape[0])).reshape(1, 2 * lanes)

    field = (quants, basis, lanes)
    table = (quants * ROWS, 4 * lanes)
    messages = [(groups[0][1] * ROWS, lanes) for groups in (DOM_GROUPS, DOM_GROUPS, SUB_GROUPS, SUB_GROUPS)]
    depth = fold_depth(basis)
    flat = quants * lanes
    folded = ((depth, flat), BF16)
    stiffened = ((3 * basis, flat), F32)
    padded = ((4 * ROWS, 128), F32)
    own_solved = ((4 * ROWS, flat), F32)
    near_solved = ((2 * 3 * 4 * ROWS, flat), F32)

    first, second, table_one, *sends = run(
        first_kernel, [field, field, table] + messages, [folded, stiffened, padded],
        state, jac, stiffness, proj, send_row,
    )
    arrived = exchange(sends)
    part_one, local_one, lifting = run(
        second_kernel, [field, table, (basis, 3 * 4 * ROWS)],
        [folded, stiffened, own_solved, padded],
        state, first, table_one, jac, stiffness, proj, rotations, flux, neighbour_slot,
    )
    middle, integral, picked_one, table_two, *sends = run(
        third_kernel, [field, field, table, table] + messages,
        [folded, stiffened, near_solved, padded],
        state, first, second, part_one, local_one, *arrived,
        jac, stiffness, proj, flux, neighbour_slot, orient, cluster, lifting, send_row,
    )
    arrived = exchange(sends)
    part_two, local_two = run(
        fourth_kernel, [field, table],
        [folded, stiffened, own_solved, padded, (table, F32)],
        middle, integral, table_one, table_two, picked_one, jac, stiffness, proj, flux,
        neighbour_slot, cluster,
    )
    updated, = run(
        fifth_kernel, [field], [near_solved, (table, F32)],
        part_two, local_two, *arrived, flux, neighbour_slot, orient, lifting, limit,
    )
    return jnp.transpose(updated, (1, 0, 2))


def solution(mesh):
    placed = (
        P(None, None, ("dom", "sub")),
        P(),
        P(None, None, None, ("dom", "sub")),
        P(None, None, None, None, ("dom", "sub")),
        P(),
        P(),
        P(("dom", "sub")),
        P(("dom", "sub")),
        P(None, ("dom", "sub")),
        P(None, ("dom", "sub")),
        P(("dom", "sub")),
    )
    return jax.shard_map(
        on_device,
        mesh=mesh,
        in_specs=placed,
        out_specs=P(None, None, ("dom", "sub")),
        check_vma=False,
    )
```

profile of v0, /device:TPU:26, one launch (start us, length us, event | category | flops | bytes accessed | tf_op | source)
XLA Modules:
  0.0 50.6 jit_solution(16410749509846003825)
XLA Ops:
  0.0 0.7 %pad.4 = s32[256]{0:T(256)S(1)} pad(s32[192]{0:T(256)} %param.21, s32[]{:T(128)} %constant.0.clone.1), padding=0_64 | pad | bytes 1796 | tf_op jit(solution)/shard_map/jit(_pad)/pad | solution.py:436
  0.7 0.9 %copy-done.1 = f32[3,9,9,128]{3,0,2,1:T(4,128)S(1)} copy-done((f32[3,9,9,128]{3,0,2,1:T(4,128)S(1)}, f32[3,9,9,128]{3,0,2,1:T(4,128)}, u32[]{:S(2)}) %copy-start.1) | copy-done | bytes 124440
  1.7 0.9 %copy-done.3 = f32[56,9,128]{2,0,1:T(8,128)S(1)} copy-done((f32[56,9,128]{2,0,1:T(8,128)S(1)}, f32[56,9,128]{2,0,1:T(8,128)}, u32[]{:S(2)}) %copy-start.3) | copy-done | bytes 258072
  2.6 0.9 %copy-done.4 = f32[3,56,56]{2,1,0:T(8,128)S(1)} copy-done((f32[3,56,56]{2,1,0:T(8,128)S(1)}, f32[3,56,56]{2,1,0:T(8,128)}, u32[]{:S(2)}) %copy-start.4) | copy-done | bytes 37656
  3.5 0.8 %copy-done.5 = f32[4,21,56]{2,0,1:T(4,128)S(1)} copy-done((f32[4,21,56]{2,0,1:T(4,128)S(1)}, f32[4,21,56]{2,0,1:T(4,128)}, u32[]{:S(2)}) %copy-start.5) | copy-done | bytes 18840
  4.3 5.4 %first_kernel.1 = (f32[9,56,128]{2,1,0:T(8,128)S(1)}, f32[9,56,128]{2,1,0:T(8,128)S(1)}, f32[216,512]{1,0:T(8,128)S(1)}, f32[120,128]{1,0:T(8,128)S(1)}, f32[120...) custom-call(f32[9,56,128]{2,1,0:T(8,128)S(1)} %bitcast.16, f32[9,9,3,128]{3,2,1,0:T(4,128)S(1)} %bitcast.12, ...), custom_call_target="tpu_custom_call" | custom-call | tf_op jit(solution)/shard_map/first_kernel/pallas_call | solution.py:389
  9.7 1.9 %collective-permute-start = (f32[120,128]{1,0:T(8,128)S(1)}, f32[120,128]{1,0:T(8,128)S(1)}, u32[]{:S(2)}, u32[]{:S(2)}) collective-permute-start(f32[120,128]{1,0:T(8,128)S(1)} %get-tuple-element.30), channel_id=1, source_target_pairs={{0,4},{4,8},{8,12},{12,16},{16,20},{20,24},{24,28},{1,5},{5,9},{9,... | collective-permute-start | bytes 184328 | tf_op jit(solution)/shard_map/ppermute | solution.py:406
  11.7 3.6 %collective-permute-start.1 = (f32[120,128]{1,0:T(8,128)S(1)}, f32[120,128]{1,0:T(8,128)S(1)}, u32[]{:S(2)}, u32[]{:S(2)}) collective-permute-start(f32[120,128]{1,0:T(8,128)S(1)} %get-tuple-element.31), channel_id=1, source_target_pairs={{4,0},{8,4},{12,8},{16,12},{20,16},{24,20},{28,24},{5,1},{9,5},{13... | collective-permute-start | bytes 184328 | tf_op jit(solution)/shard_map/ppermute | solution.py:406
  15.3 3.4 %collective-permute-start.2 = (f32[72,128]{1,0:T(8,128)S(1)}, f32[72,128]{1,0:T(8,128)S(1)}, u32[]{:S(2)}, u32[]{:S(2)}) collective-permute-start(f32[72,128]{1,0:T(8,128)S(1)} %get-tuple-element.32), channel_id=1, source_target_pairs={{0,1},{1,2},{2,3},{4,5},{5,6},{6,7},{8,9},{9,10},{10,11},{12,13},{... | collective-permute-start | bytes 110600 | tf_op jit(solution)/shard_map/ppermute | solution.py:406
  18.7 2.4 %collective-permute-start.3 = (f32[72,128]{1,0:T(8,128)S(1)}, f32[72,128]{1,0:T(8,128)S(1)}, u32[]{:S(2)}, u32[]{:S(2)}) collective-permute-start(f32[72,128]{1,0:T(8,128)S(1)} %get-tuple-element.33), channel_id=1, source_target_pairs={{1,0},{2,1},{3,2},{5,4},{6,5},{7,6},{9,8},{10,9},{11,10},{13,12},{... | collective-permute-start | bytes 110600 | tf_op jit(solution)/shard_map/ppermute | solution.py:406
  21.2 0.0 copy-start.7
  21.2 0.0 copy-done
  21.2 0.7 %copy-done.7 = s32[4,128]{1,0:T(4,128)S(1)} copy-done((s32[4,128]{1,0:T(4,128)S(1)}, s32[4,128]{1,0:T(4,128)}, u32[]{:S(2)}) %copy-start.7) | copy-done | bytes 2072
  21.8 2.3 %second_kernel.1 = (f32[9,56,128]{2,1,0:T(8,128)S(1)}, f32[216,512]{1,0:T(8,128)S(1)}, f32[56,288]{1,0:T(8,128)S(1)}) custom-call(f32[9,56,128]{2,1,0:T(8,128)S(1)} %bitcast.17, f32[9,56,128]{2,1,0:T(8,128)S(1)} %get-tuple-element.25.first, f32[216,512]{1,0:T(8,128)S(1)} %get-tuple-element.27.table.table_one, f32[9,9,3,128]{3,2,1,0:T(4,128)S(1)} %bitcast.13, ...), custom_call_target="tpu_custom_call" | custom-call | tf_op jit(solution)/shard_map/second_kernel/pallas_call | solution.py:389
  24.1 0.0 collective-permute-done.2.from_left
  24.1 1.3 %collective-permute-done.3.from_right = f32[72,128]{1,0:T(8,128)S(1)} collective-permute-done((f32[72,128]{1,0:T(8,128)S(1)}, f32[72,128]{1,0:T(8,128)S(1)}, u32[]{:S(2)}, u32[]{:S(2)}) %collective-permute-start.3) | collective-permute-done | bytes 36896 | tf_op jit(solution)/shard_map/ppermute | solution.py:406
  25.5 0.0 collective-permute-done.from_lower
  25.5 0.0 collective-permute-done.1.from_upper
  25.5 0.0 copy-start.9
  25.5 0.7 %copy-done.8 = s32[4,128]{1,0:T(4,128)S(1)} copy-done((s32[4,128]{1,0:T(4,128)S(1)}, s32[4,128]{1,0:T(4,128)}, u32[]{:S(2)}) %copy-start.8) | copy-done | bytes 2072
  26.2 6.4 %third_kernel.1 = (f32[9,56,128]{2,1,0:T(8,128)S(1)}, f32[9,56,128]{2,1,0:T(8,128)S(1)}, f32[216,512]{1,0:T(8,128)S(1)}, f32[216,512]{1,0:T(8,128)S(1)}, f32[120...) custom-call(f32[9,56,128]{2,1,0:T(8,128)S(1)} %bitcast.18, ...), custom_call_target="tpu_custom_call" | custom-call | tf_op jit(solution)/shard_map/third_kernel/pallas_call | solution.py:389
  32.6 1.9 %collective-permute-start.4 = (f32[120,128]{1,0:T(8,128)S(1)}, f32[120,128]{1,0:T(8,128)S(1)}, u32[]{:S(2)}, u32[]{:S(2)}) collective-permute-start(f32[120,128]{1,0:T(8,128)S(1)} %get-tuple-element.41), channel_id=1, source_target_pairs={{0,4},{4,8},{8,12},{12,16},{16,20},{20,24},{24,28},{1,5},{5,9},{9,... | collective-permute-start | bytes 184328 | tf_op jit(solution)/shard_map/ppermute | solution.py:406
  34.5 3.6 %collective-permute-start.5 = (f32[120,128]{1,0:T(8,128)S(1)}, f32[120,128]{1,0:T(8,128)S(1)}, u32[]{:S(2)}, u32[]{:S(2)}) collective-permute-start(f32[120,128]{1,0:T(8,128)S(1)} %get-tuple-element.42), channel_id=1, source_target_pairs={{4,0},{8,4},{12,8},{16,12},{20,16},{24,20},{28,24},{5,1},{9,5},{13... | collective-permute-start | bytes 184328 | tf_op jit(solution)/shard_map/ppermute | solution.py:406
  38.1 3.0 %collective-permute-start.6 = (f32[72,128]{1,0:T(8,128)S(1)}, f32[72,128]{1,0:T(8,128)S(1)}, u32[]{:S(2)}, u32[]{:S(2)}) collective-permute-start(f32[72,128]{1,0:T(8,128)S(1)} %get-tuple-element.43), channel_id=1, source_target_pairs={{0,1},{1,2},{2,3},{4,5},{5,6},{6,7},{8,9},{9,10},{10,11},{12,13},{... | collective-permute-start | bytes 110600 | tf_op jit(solution)/shard_map/ppermute | solution.py:406
  41.1 2.9 %collective-permute-start.7 = (f32[72,128]{1,0:T(8,128)S(1)}, f32[72,128]{1,0:T(8,128)S(1)}, u32[]{:S(2)}, u32[]{:S(2)}) collective-permute-start(f32[72,128]{1,0:T(8,128)S(1)} %get-tuple-element.44), channel_id=1, source_target_pairs={{1,0},{2,1},{3,2},{5,4},{6,5},{7,6},{9,8},{10,9},{11,10},{13,12},{... | collective-permute-start | bytes 110600 | tf_op jit(solution)/shard_map/ppermute | solution.py:406
  44.0 1.6 %fourth_kernel.1 = (f32[9,56,128]{2,1,0:T(8,128)S(1)}, f32[216,512]{1,0:T(8,128)S(1)}) custom-call(f32[9,56,128]{2,1,0:T(8,128)S(1)} %get-tuple-element.35.middle, f32[9,56,128]{2,1,0:T(8,128)S(1)} %get-tuple-element.36.integral, f32[216,512]{1,0:T(8,128)S(1)} %get-tuple-element.27.table.table_one, f32[216,512]{1,0:T(8,128)S(1)} %get-tuple-element.37.table_two, ...), custom_call_target="tpu_custom_call" | custom-call | tf_op jit(solution)/shard_map/fourth_kernel/pallas_call | solution.py:389
  45.7 0.0 collective-permute-done.6.from_left
  45.7 2.2 %collective-permute-done.7.from_right = f32[72,128]{1,0:T(8,128)S(1)} collective-permute-done((f32[72,128]{1,0:T(8,128)S(1)}, f32[72,128]{1,0:T(8,128)S(1)}, u32[]{:S(2)}, u32[]{:S(2)}) %collective-permute-start.7) | collective-permute-done | bytes 36896 | tf_op jit(solution)/shard_map/ppermute | solution.py:406
  47.9 0.0 collective-permute-done.4.from_lower
  47.9 0.0 collective-permute-done.5.from_upper
  47.9 0.7 %copy-done.10 = f32[128]{0:T(128)S(1)} copy-done((f32[128]{0:T(128)S(1)}, f32[128]{0:T(128)}, u32[]{:S(2)}) %copy-start.10) | copy-done | bytes 536
  48.5 2.0 %fifth_kernel.1 = f32[9,56,128]{2,1,0:T(8,128)} custom-call(f32[9,56,128]{2,1,0:T(8,128)S(1)} %get-tuple-element.39.part, f32[216,512]{1,0:T(8,128)S(1)} %get-tuple-element.40.picked_local, f32[120,128]{1,0:T(8,128)S(1)} %collective-permute-done.4.from_lower, f32[120,128]{1,0:T(8,128)S(1)} %collective-permute-done.5.from_upper, ...), custom_call_target="tpu_custom_call" | custom-call | tf_op jit(solution)/shard_map/fifth_kernel/pallas_call | solution.py:389
  (12 shorter events, 0.0 us)
Async XLA Ops:
  0.0 21.2 %copy-start = (f32[2,4,9,9,128]{4,1,3,2,0:T(4,128)S(1)}, f32[2,4,9,9,128]{4,1,3,2,0:T(4,128)}, u32[]{:S(2)}) copy-start(f32[2,4,9,9,128]{4,1,3,2,0:T(4,128)} %param.14) | copy-start | bytes 995332
  0.7 0.9 %copy-start.1 = (f32[3,9,9,128]{3,0,2,1:T(4,128)S(1)}, f32[3,9,9,128]{3,0,2,1:T(4,128)}, u32[]{:S(2)}) copy-start(f32[3,9,9,128]{3,0,2,1:T(4,128)} %param.13) | copy-start | bytes 373252
  1.6 0.9 %copy-start.3 = (f32[56,9,128]{2,0,1:T(8,128)S(1)}, f32[56,9,128]{2,0,1:T(8,128)}, u32[]{:S(2)}) copy-start(f32[56,9,128]{2,0,1:T(8,128)} %param.11) | copy-start | bytes 774148
  2.6 0.9 %copy-start.4 = (f32[3,56,56]{2,1,0:T(8,128)S(1)}, f32[3,56,56]{2,1,0:T(8,128)}, u32[]{:S(2)}) copy-start(f32[3,56,56]{2,1,0:T(8,128)} %stiffness.7) | copy-start | bytes 112900
  3.5 0.8 %copy-start.5 = (f32[4,21,56]{2,0,1:T(4,128)S(1)}, f32[4,21,56]{2,0,1:T(4,128)}, u32[]{:S(2)}) copy-start(f32[4,21,56]{2,0,1:T(4,128)} %param.15) | copy-start | bytes 56452
  4.3 16.9 %copy-start.6 = (f32[3,21,21]{2,1,0:T(8,128)S(1)}, f32[3,21,21]{2,1,0:T(8,128)}, u32[]{:S(2)}) copy-start(f32[3,21,21]{2,1,0:T(8,128)} %rotations.1) | copy-start | bytes 15880
  9.7 15.7 %collective-permute-start = (f32[120,128]{1,0:T(8,128)S(1)}, f32[120,128]{1,0:T(8,128)S(1)}, u32[]{:S(2)}, u32[]{:S(2)}) collective-permute-start(f32[120,128]{1,0:T(8,128)S(1)} %get-tuple-element.30), channel_id=1, source_target_pairs={{0,4},{4,8},{8,12},{12,16},{16,20},{20,24},{24,28},{1,5},{5,9},{9,... | collective-permute-start | bytes 184328 | tf_op jit(solution)/shard_map/ppermute | solution.py:406
  11.7 13.8 %collective-permute-start.1 = (f32[120,128]{1,0:T(8,128)S(1)}, f32[120,128]{1,0:T(8,128)S(1)}, u32[]{:S(2)}, u32[]{:S(2)}) collective-permute-start(f32[120,128]{1,0:T(8,128)S(1)} %get-tuple-element.31), channel_id=1, source_target_pairs={{4,0},{8,4},{12,8},{16,12},{20,16},{24,20},{28,24},{5,1},{9,5},{13... | collective-permute-start | bytes 184328 | tf_op jit(solution)/shard_map/ppermute | solution.py:406
  15.3 8.8 %collective-permute-start.2 = (f32[72,128]{1,0:T(8,128)S(1)}, f32[72,128]{1,0:T(8,128)S(1)}, u32[]{:S(2)}, u32[]{:S(2)}) collective-permute-start(f32[72,128]{1,0:T(8,128)S(1)} %get-tuple-element.32), channel_id=1, source_target_pairs={{0,1},{1,2},{2,3},{4,5},{5,6},{6,7},{8,9},{9,10},{10,11},{12,13},{... | collective-permute-start | bytes 110600 | tf_op jit(solution)/shard_map/ppermute | solution.py:406
  18.7 6.8 %collective-permute-start.3 = (f32[72,128]{1,0:T(8,128)S(1)}, f32[72,128]{1,0:T(8,128)S(1)}, u32[]{:S(2)}, u32[]{:S(2)}) collective-permute-start(f32[72,128]{1,0:T(8,128)S(1)} %get-tuple-element.33), channel_id=1, source_target_pairs={{1,0},{2,1},{3,2},{5,4},{6,5},{7,6},{9,8},{10,9},{11,10},{13,12},{... | collective-permute-start | bytes 110600 | tf_op jit(solution)/shard_map/ppermute | solution.py:406
  21.2 0.7 %copy-start.7 = (s32[4,128]{1,0:T(4,128)S(1)}, s32[4,128]{1,0:T(4,128)}, u32[]{:S(2)}) copy-start(s32[4,128]{1,0:T(4,128)} %slot.7) | copy-start | bytes 6148
  25.5 0.7 %copy-start.8 = (s32[4,128]{1,0:T(4,128)S(1)}, s32[4,128]{1,0:T(4,128)}, u32[]{:S(2)}) copy-start(s32[4,128]{1,0:T(4,128)} %orient.3) | copy-start | bytes 6148
  25.5 0.7 %copy-start.9 = (s32[128]{0:T(128)S(1)}, s32[128]{0:T(128)}, u32[]{:S(2)}) copy-start(s32[128]{0:T(128)} %param.18) | copy-start | bytes 1540
  26.2 17.8 %copy-start.2 = (f32[3,9,9,128]{3,0,2,1:T(4,128)S(1)}, f32[3,9,9,128]{3,0,2,1:T(4,128)}, u32[]{:S(2)}) copy-start(f32[3,9,9,128]{3,0,2,1:T(4,128)} %param.13) | copy-start | bytes 373252
  32.6 15.3 %collective-permute-start.4 = (f32[120,128]{1,0:T(8,128)S(1)}, f32[120,128]{1,0:T(8,128)S(1)}, u32[]{:S(2)}, u32[]{:S(2)}) collective-permute-start(f32[120,128]{1,0:T(8,128)S(1)} %get-tuple-element.41), channel_id=1, source_target_pairs={{0,4},{4,8},{8,12},{12,16},{16,20},{20,24},{24,28},{1,5},{5,9},{9,... | collective-permute-start | bytes 184328 | tf_op jit(solution)/shard_map/ppermute | solution.py:406
  34.5 13.4 %collective-permute-start.5 = (f32[120,128]{1,0:T(8,128)S(1)}, f32[120,128]{1,0:T(8,128)S(1)}, u32[]{:S(2)}, u32[]{:S(2)}) collective-permute-start(f32[120,128]{1,0:T(8,128)S(1)} %get-tuple-element.42), channel_id=1, source_target_pairs={{4,0},{8,4},{12,8},{16,12},{20,16},{24,20},{28,24},{5,1},{9,5},{13... | collective-permute-start | bytes 184328 | tf_op jit(solution)/shard_map/ppermute | solution.py:406
  38.1 7.5 %collective-permute-start.6 = (f32[72,128]{1,0:T(8,128)S(1)}, f32[72,128]{1,0:T(8,128)S(1)}, u32[]{:S(2)}, u32[]{:S(2)}) collective-permute-start(f32[72,128]{1,0:T(8,128)S(1)} %get-tuple-element.43), channel_id=1, source_target_pairs={{0,1},{1,2},{2,3},{4,5},{5,6},{6,7},{8,9},{9,10},{10,11},{12,13},{... | collective-permute-start | bytes 110600 | tf_op jit(solution)/shard_map/ppermute | solution.py:406
  41.1 6.8 %collective-permute-start.7 = (f32[72,128]{1,0:T(8,128)S(1)}, f32[72,128]{1,0:T(8,128)S(1)}, u32[]{:S(2)}, u32[]{:S(2)}) collective-permute-start(f32[72,128]{1,0:T(8,128)S(1)} %get-tuple-element.44), channel_id=1, source_target_pairs={{1,0},{2,1},{3,2},{5,4},{6,5},{7,6},{9,8},{10,9},{11,10},{13,12},{... | collective-permute-start | bytes 110600 | tf_op jit(solution)/shard_map/ppermute | solution.py:406
  47.9 0.7 %copy-start.10 = (f32[128]{0:T(128)S(1)}, f32[128]{0:T(128)}, u32[]{:S(2)}) copy-start(f32[128]{0:T(128)} %param.17) | copy-start | bytes 1540
where the time goes:
time: 51.1 us; the launch traced here: 50.6 us
  starting transfers between devices  22.8 us (45%)
  Pallas kernels  17.8 us (35%)
  local copies, waits for them, and re-layouts  6.26 us (12%)
  waiting for transfers between devices  3.58 us (7%)
    ppermute x8, starting transfers between devices, shift(): return lax.ppermute(value, axis, pairs)  22.8 us
    pallas_call x5, Pallas kernels, run(): pl.pallas_call(body, out_shape=[jax.ShapeDtypeStruct(shape, F32) for shap...  17.8 us
    unnamed x22, local copies, waits for them, and re-layouts  5.53 us
    ppermute x8, waiting for transfers between devices, shift(): return lax.ppermute(value, axis, pairs)  3.58 us
  transfers between devices with their start and end apart: 8, of which 2 were waited for; matrix products, arithmetic and copies ran while one was open for 0% of the time, Pallas kernels for 8%

commit v1 on v0

--- a/solution.py
+++ b/solution.py
@@ -17,6 +17,10 @@
 
 DOM_GROUPS = ((0, 5), (5, 4))
 SUB_GROUPS = ((0, 3), (3, 2), (5, 2), (7, 2))
+
+GRANT = 32
+INPUTS = 11
+FIRST_USED = 5
 
 
 def iota(shape, dim):
@@ -123,49 +127,70 @@
             ]
 
 
+def grid_spot():
+    i, j = lax.axis_index("dom"), lax.axis_index("sub")
+    return (
+        lax.rem(i, 2), lax.rem(j, 2),
+        i > 0, i < lax.axis_size("dom") - 1, j > 0, j < lax.axis_size("sub") - 1,
+    )
+
+
+def partners(parity_dom, parity_sub, tiling):
+    u = parity_dom if tiling == 0 else 1 - parity_dom
+    v = parity_sub if tiling == 0 else 1 - parity_sub
+    return (1 - u) * 2 + v, u * 2 + (1 - v)
+
+
 def pick_sends(table, send_row, outs, lanes):
     faces = table.shape[1]
+    parity_dom, parity_sub, *_ = grid_spot()
     low = jnp.broadcast_to(send_row[:, 0:lanes], (8, lanes))
     lane = iota((8, lanes), 1)
     turned = pltpu.roll(low, SLOTS_DOM, 1)
-    high = jnp.broadcast_to(send_row[:, lanes:2 * lanes], (8, lanes))
+    to_lower = jnp.where(lane < SLOTS_DOM, low, turned)
+    to_upper = jnp.where(lane < SLOTS_DOM, turned, low)
+    high = send_row[:, 2 * SLOTS_DOM:2 * SLOTS_DOM + 2 * SLOTS_SUB]
+    spread = jnp.broadcast_to(jnp.concatenate([high, high], axis=1), (8, lanes))
+    moved = pltpu.roll(spread, SLOTS_SUB, 1)
+    left = lax.rem(lane, 2 * SLOTS_SUB) < SLOTS_SUB
+    to_left = jnp.where(left, spread, moved)
+    to_right = jnp.where(left, moved, spread)
+    even_dom, even_sub = parity_dom == 0, parity_sub == 0
     pieces = [
-        jnp.where(lane < SLOTS_DOM, low, turned),
-        jnp.where(lane < SLOTS_DOM, turned, low),
+        jnp.where(even_dom, to_upper, to_lower),
+        jnp.where(even_dom, to_lower, to_upper),
+        jnp.where(even_sub, to_right, to_left),
+        jnp.where(even_sub, to_left, to_right),
     ]
-    spread = jnp.where(lane < 2 * SLOTS_SUB, high, pltpu.roll(high, 2 * SLOTS_SUB, 1))
-    moved = pltpu.roll(spread, SLOTS_SUB, 1)
-    even = lax.rem(lane, 2 * SLOTS_SUB) < SLOTS_SUB
-    pieces += [jnp.where(even, spread, moved), jnp.where(even, moved, spread)]
     index = jnp.concatenate([piece[0:1] for piece in pieces], axis=1)
     chosen = one_hot(index, 0, faces)
     upper, lower = halves(table[...])
     sent = dot(upper, chosen) + dot(lower, chosen)
-    for k, (out, groups) in enumerate(
-        zip(outs, (DOM_GROUPS, DOM_GROUPS, SUB_GROUPS, SUB_GROUPS))
-    ):
+    for k, groups in enumerate((DOM_GROUPS, DOM_GROUPS, SUB_GROUPS, SUB_GROUPS)):
+        out = outs[k % 2]
+        place = partners(parity_dom, parity_sub, k % 2)[k // 2]
         width = lanes // len(groups)
         values = sent[:, k * lanes:(k + 1) * lanes]
         start, count = groups[0]
         packed = values[0:count * ROWS]
         least = min(count for _, count in groups) * ROWS
-        place = iota((least, lanes), 1)
+        spot = iota((least, lanes), 1)
         head = packed[0:least]
         for g, (start, _) in enumerate(groups):
             if g:
                 head = jnp.where(
-                    place >= g * width, values[start * ROWS:start * ROWS + least], head
+                    spot >= g * width, values[start * ROWS:start * ROWS + least], head
                 )
-        out[0:least] = head
-        out[least:count * ROWS] = packed[least:]
-
-
-def spread_received(arrived, groups, lanes):
+        out[place, 0:least] = head
+        out[place, least:count * ROWS] = packed[least:]
+
+
+def spread_received(arrived, valid, groups, lanes):
     width = lanes // len(groups)
     parts = []
     for g, (_, count) in enumerate(groups):
         place = iota((count * ROWS, lanes), 1)
-        mine = (place >= g * width) & (place < (g + 1) * width)
+        mine = (place >= g * width) & (place < (g + 1) * width) & valid
         parts.append(jnp.where(mine, arrived[0:count * ROWS], 0.0))
     return jnp.concatenate(parts, axis=0)
 
@@ -177,21 +202,39 @@
 
 
 def pick_received(arrived, slot, faces, lanes):
+    parity_dom, parity_sub, lower, upper, left, right = grid_spot()
+    even_dom, even_sub = parity_dom == 0, parity_sub == 0
+    starts = (faces, faces + SLOTS_DOM, faces + 2 * SLOTS_DOM, faces + 2 * SLOTS_DOM + SLOTS_SUB)
+    true = parity_dom >= 0
+    firsts = (
+        jnp.where(even_dom, starts[1], starts[0]), jnp.where(even_dom, starts[0], starts[1]),
+        jnp.where(even_sub, starts[3], starts[2]), jnp.where(even_sub, starts[2], starts[3]),
+    )
+    valid = (
+        true, (even_dom & lower) | (~even_dom & upper),
+        true, (even_sub & left) | (~even_sub & right),
+    )
+    widths = (SLOTS_DOM, SLOTS_DOM, SLOTS_SUB, SLOTS_SUB)
+    all_groups = (DOM_GROUPS, DOM_GROUPS, SUB_GROUPS, SUB_GROUPS)
     spread = jnp.concatenate(
         [
-            spread_received(item[...], groups, lanes)
-            for item, groups in zip(arrived, (DOM_GROUPS, DOM_GROUPS, SUB_GROUPS, SUB_GROUPS))
+            spread_received(
+                arrived[k % 2][
+                    partners(parity_dom, parity_sub, k % 2)[k // 2],
+                    0:groups[0][1] * ROWS,
+                ],
+                valid[k], groups, lanes,
+            )
+            for k, groups in enumerate(all_groups)
         ],
         axis=1,
     )
-    starts = (faces, faces + SLOTS_DOM, faces + 2 * SLOTS_DOM, faces + 2 * SLOTS_DOM + SLOTS_SUB)
-    widths = (SLOTS_DOM, SLOTS_DOM, SLOTS_SUB, SLOTS_SUB)
     chosen = jnp.concatenate(
         [
             jnp.concatenate(
                 [one_hot(slot[f:f + 1], first, lanes, width) for f in range(4)], axis=1
             )
-            for first, width in zip(starts, widths)
+            for first, width in zip(firsts, widths)
         ],
         axis=0,
     )
@@ -205,13 +248,12 @@
 
 
 def local_update(
-    base, integral, table, jac, stiffness, flux, lifting, folded, stiffened, solved, write,
+    base, integral, table, jac, turned_fold, flux, lifting, folded, stiffened, solved, write,
     basis, quants, lanes,
 ):
     for q in range(quants):
         folded[:, q * lanes:(q + 1) * lanes] = fold_rows(integral(q))
-    turned = jnp.concatenate([stiffness[d].T for d in range(3)], axis=0)
-    stiffened[...] = dot(fold_columns(turned), folded[...])
+    stiffened[...] = dot(turned_fold, folded[...])
 
     def keep(f, p, total):
         solved[f * ROWS:(f + 1) * ROWS, p * lanes:(p + 1) * lanes] = total
@@ -258,11 +300,20 @@
     return exact_dot(own_lifting, jnp.where(same, tall, 0.0))
 
 
-def first_kernel(
-    state, jac, stiffness, projector, send_row,
-    first, second, table, to_lower, to_upper, to_left, to_right,
-    folded, stiffened, padded,
-):
+def first_kernel(*refs):
+    inputs, refs = refs[:INPUTS], refs[INPUTS:]
+    held, refs = refs[:INPUTS], refs[INPUTS:]
+    (first, second, table, padded, stiff_fold, send_even, send_odd,
+     folded, stiffened, arrivals) = refs
+    copies = [
+        pltpu.make_async_copy(source, target, arrivals.at[k])
+        for k, (source, target) in enumerate(zip(inputs, held))
+    ]
+    for copy in copies:
+        copy.start()
+    state, stiffness, projector, jac, send_row = held[:FIRST_USED]
+    for copy in copies[:FIRST_USED]:
+        copy.wait()
     quants, basis, lanes = state.shape
     for q in range(quants):
         value = state[q]
@@ -271,22 +322,26 @@
         folded[:, q * lanes:(q + 1) * lanes] = fold_rows(value)
     fill_projector(projector, padded)
     stacked = jnp.concatenate([stiffness[d] for d in range(3)], axis=0)
-    predict(
-        fold_columns(stacked), jac, folded, stiffened, first, second, basis, quants, lanes
-    )
+    fold = fold_columns(stacked)
+    stiff_fold[...] = fold.astype(F32)
+    predict(fold, jac, folded, stiffened, first, second, basis, quants, lanes)
     for q in range(quants):
         folded[:, q * lanes:(q + 1) * lanes] = fold_rows(first[q])
     project_table(padded, folded, table, basis, quants, lanes)
-    pick_sends(table, send_row, (to_lower, to_upper, to_left, to_right), lanes)
+    pick_sends(table, send_row, (send_even, send_odd), lanes)
+    for copy in copies[FIRST_USED:]:
+        copy.wait()
 
 
 def second_kernel(
-    state, first, table, jac, stiffness, projector, rotations, flux, slot,
-    part, picked, lifting,
-    folded, stiffened, solved, padded,
+    state, first, table, jac, stiffness, padded, rotations, flux, slot,
+    part, picked, lifting, turned_fold,
+    folded, stiffened, solved,
 ):
     quants, basis, lanes = state.shape
-    fill_projector(projector, padded)
+    turned = jnp.concatenate([stiffness[d].T for d in range(3)], axis=0)
+    fold = fold_columns(turned)
+    turned_fold[...] = fold.astype(F32)
     own_lifting = padded[...].T[0:basis]
     lifting[...] = near_lifting(own_lifting, rotations)
     picked[...] = pick_local(table[...], slot, 4 * lanes)
@@ -295,21 +350,20 @@
         part[p] = value
 
     local_update(
-        lambda p: state[p], lambda q: first[q], table, jac, stiffness, flux, own_lifting,
+        lambda p: state[p], lambda q: first[q], table, jac, fold, flux, own_lifting,
         folded, stiffened, solved, write, basis, quants, lanes,
     )
 
 
 def third_kernel(
-    state, first, second, part, picked_local, from_lower, from_upper, from_left, from_right,
-    jac, stiffness, projector, flux, slot, orient, cluster, lifting, send_row,
-    middle, integral, picked, table, to_lower, to_upper, to_left, to_right,
-    folded, stiffened, solved, padded,
+    state, first, second, part, picked_local, from_even, from_odd,
+    jac, stiff_fold, padded, flux, slot, orient, cluster, lifting, send_row,
+    middle, integral, picked, table, send_even, send_odd,
+    folded, stiffened, solved,
 ):
     quants, basis, lanes = state.shape
-    fill_projector(projector, padded)
     picked[...] = picked_local[...] + pick_received(
-        (from_lower, from_upper, from_left, from_right), slot, 4 * lanes, lanes
+        (from_even, from_odd), slot, 4 * lanes, lanes
     )
     near = near_lift(picked, flux, orient, lifting[...], solved, quants, lanes)
     fine = cluster[...] == 0
@@ -318,9 +372,9 @@
         middle[q] = value
         integral[q] = value
         folded[:, q * lanes:(q + 1) * lanes] = fold_rows(value)
-    stacked = jnp.concatenate([stiffness[d] for d in range(3)], axis=0)
     predict(
-        fold_columns(stacked), jac, folded, stiffened, integral, None, basis, quants, lanes
+        stiff_fold[...].astype(BF16), jac, folded, stiffened, integral, None,
+        basis, quants, lanes,
     )
     for q in range(quants):
         fine_first = integral[q]
@@ -328,17 +382,16 @@
         folded[:, q * lanes:(q + 1) * lanes] = fold_rows(late)
         integral[q] = jnp.where(fine, fine_first, first[q] + second[q])
     project_table(padded, folded, table, basis, quants, lanes)
-    pick_sends(table, send_row, (to_lower, to_upper, to_left, to_right), lanes)
+    pick_sends(table, send_row, (send_even, send_odd), lanes)
 
 
 def fourth_kernel(
-    middle, integral, table_one, table_two, picked_one, jac, stiffness, projector, flux, slot,
+    middle, integral, table_one, table_two, picked_one, jac, turned_fold, padded, flux, slot,
     cluster,
     part, picked,
-    folded, stiffened, solved, padded, total_table,
+    folded, stiffened, solved, total_table,
 ):
     quants, basis, lanes = middle.shape
-    fill_projector(projector, padded)
     own_lifting = padded[...].T[0:basis]
     coarse = jnp.concatenate([cluster[...] != 0] * 4, axis=1)
     total_table[...] = table_two[...] + jnp.where(coarse, table_one[...], 0.0)
@@ -350,20 +403,20 @@
         part[p] = value
 
     local_update(
-        lambda p: middle[p], lambda q: integral[q], total_table, jac, stiffness, flux,
+        lambda p: middle[p], lambda q: integral[q], total_table, jac, turned_fold[...].astype(BF16), flux,
         own_lifting, folded, stiffened, solved, write, basis, quants, lanes,
     )
 
 
 def fifth_kernel(
-    part, picked_local, from_lower, from_upper, from_left, from_right, flux, slot, orient,
-    lifting, yield_stress,
+    part, picked_local, from_even, from_odd, flux, slot, orient, lifting,
+    yield_stress,
     updated,
     solved, picked,
 ):
     quants, basis, lanes = part.shape
     picked[...] = picked_local[...] + pick_received(
-        (from_lower, from_upper, from_left, from_right), slot, 4 * lanes, lanes
+        (from_even, from_odd), slot, 4 * lanes, lanes
     )
     near = near_lift(picked, flux, orient, lifting[...], solved, quants, lanes)
     stepped = [part[q] - near[:, q * lanes:(q + 1) * lanes] for q in range(quants)]
@@ -384,33 +437,38 @@
         updated[q] = stepped[q]
 
 
-def run(body, outs, scratch, *operands):
+def run(body, outs, scratch, *operands, space=pltpu.VMEM, grant=32):
     vmem = pl.BlockSpec(memory_space=pltpu.VMEM)
     return pl.pallas_call(
         body,
-        out_shape=[jax.ShapeDtypeStruct(shape, F32) for shape in outs],
-        in_specs=[vmem] * len(operands),
+        out_shape=[
+            out if isinstance(out, jax.ShapeDtypeStruct) else jax.ShapeDtypeStruct(out, F32)
+            for out in outs
+        ],
+        in_specs=[pl.BlockSpec(memory_space=space)] * len(operands),
         out_specs=[vmem] * len(outs),
-        scratch_shapes=[pltpu.VMEM(shape, kind) for shape, kind in scratch],
-        compiler_params=pltpu.CompilerParams(vmem_limit_bytes=32 * 1024 * 1024),
+        scratch_shapes=scratch,
+        compiler_params=pltpu.CompilerParams(vmem_limit_bytes=grant * 1024 * 1024),
         name=body.__name__,
     )(*operands)
 
 
+def blocks(shift):
+    rows, columns = lax.axis_size("dom"), lax.axis_size("sub")
+    groups = []
+    for i in range(shift, rows + shift, 2):
+        for j in range(shift, columns + shift, 2):
+            groups.append(
+                [(i + u) % rows * columns + (j + v) % columns for u in (0, 1) for v in (0, 1)]
+            )
+    return groups
+
+
 def exchange(sends):
-    to_lower, to_upper, to_left, to_right = sends
-
-    def shift(value, axis, step):
-        size = lax.axis_size(axis)
-        pairs = [(i, i + step) for i in range(size) if 0 <= i + step < size]
-        return lax.ppermute(value, axis, pairs)
-
-    return (
-        shift(to_upper, "dom", 1),
-        shift(to_lower, "dom", -1),
-        shift(to_right, "sub", 1),
-        shift(to_left, "sub", -1),
-    )
+    return [
+        lax.all_to_all(value, ("dom", "sub"), 0, 0, axis_index_groups=blocks(shift))
+        for shift, value in enumerate(sends)
+    ]
 
 
 def on_device(
@@ -427,51 +485,63 @@
     send_map,
 ):
     basis, quants, lanes = modal_state.shape
-    state = jnp.transpose(modal_state, (1, 0, 2))
-    jac = jnp.transpose(jacobians, (1, 2, 0, 3))
-    flux = jnp.transpose(flux_solvers, (0, 2, 3, 1, 4))
-    proj = jnp.transpose(projector, (1, 0, 2))
-    cluster = cluster.reshape(1, lanes)
-    limit = yield_stress.reshape(1, lanes)
-    send_row = jnp.pad(send_map, (0, 2 * lanes - send_map.shape[0])).reshape(1, 2 * lanes)
+    inputs = [
+        jnp.transpose(modal_state, (1, 0, 2)),
+        stiffness,
+        jnp.transpose(projector, (1, 0, 2)),
+        jnp.transpose(jacobians, (1, 2, 0, 3)),
+        send_map.reshape(1, -1),
+        jnp.transpose(flux_solvers, (0, 2, 3, 1, 4)),
+        rotations,
+        neighbour_slot,
+        orient,
+        cluster.reshape(1, lanes),
+        yield_stress.reshape(1, lanes),
+    ]
+    inputs = [pltpu.with_memory_space_constraint(item, pltpu.HBM) for item in inputs]
+    held = [jax.ShapeDtypeStruct(item.shape, item.dtype) for item in inputs]
 
     field = (quants, basis, lanes)
     table = (quants * ROWS, 4 * lanes)
-    messages = [(groups[0][1] * ROWS, lanes) for groups in (DOM_GROUPS, DOM_GROUPS, SUB_GROUPS, SUB_GROUPS)]
+    message = (4, DOM_GROUPS[0][1] * ROWS, lanes)
     depth = fold_depth(basis)
     flat = quants * lanes
-    folded = ((depth, flat), BF16)
-    stiffened = ((3 * basis, flat), F32)
-    padded = ((4 * ROWS, 128), F32)
-    own_solved = ((4 * ROWS, flat), F32)
-    near_solved = ((2 * 3 * 4 * ROWS, flat), F32)
-
-    first, second, table_one, *sends = run(
-        first_kernel, [field, field, table] + messages, [folded, stiffened, padded],
-        state, jac, stiffness, proj, send_row,
-    )
+    fold = (3 * basis, depth)
+    folded = pltpu.VMEM((depth, flat), BF16)
+    stiffened = pltpu.VMEM((3 * basis, flat), F32)
+    own_solved = pltpu.VMEM((4 * ROWS, flat), F32)
+    near_solved = pltpu.VMEM((2 * 3 * 4 * ROWS, flat), F32)
+
+    outs = run(
+        first_kernel,
+        held + [field, field, table, (4 * ROWS, 128), fold, message, message],
+        [folded, stiffened, pltpu.SemaphoreType.DMA((INPUTS,))],
+        *inputs, space=pl.ANY, grant=GRANT,
+    )
+    state, stiff, _, jac, send_row, flux, turns, slot, orient, cluster, limit = outs[:INPUTS]
+    first, second, table_one, padded, stiff_fold, *sends = outs[INPUTS:]
     arrived = exchange(sends)
-    part_one, local_one, lifting = run(
-        second_kernel, [field, table, (basis, 3 * 4 * ROWS)],
-        [folded, stiffened, own_solved, padded],
-        state, first, table_one, jac, stiffness, proj, rotations, flux, neighbour_slot,
+    part_one, local_one, lifting, turned_fold = run(
+        second_kernel, [field, table, (basis, 3 * 4 * ROWS), fold],
+        [folded, stiffened, own_solved],
+        state, first, table_one, jac, stiff, padded, turns, flux, slot,
     )
     middle, integral, picked_one, table_two, *sends = run(
-        third_kernel, [field, field, table, table] + messages,
-        [folded, stiffened, near_solved, padded],
+        third_kernel, [field, field, table, table, message, message],
+        [folded, stiffened, near_solved],
         state, first, second, part_one, local_one, *arrived,
-        jac, stiffness, proj, flux, neighbour_slot, orient, cluster, lifting, send_row,
+        jac, stiff_fold, padded, flux, slot, orient, cluster, lifting, send_row,
     )
     arrived = exchange(sends)
     part_two, local_two = run(
         fourth_kernel, [field, table],
-        [folded, stiffened, own_solved, padded, (table, F32)],
-        middle, integral, table_one, table_two, picked_one, jac, stiffness, proj, flux,
-        neighbour_slot, cluster,
+        [folded, stiffened, own_solved, pltpu.VMEM(table, F32)],
+        middle, integral, table_one, table_two, picked_one, jac, turned_fold, padded, flux,
+        slot, cluster,
     )
     updated, = run(
-        fifth_kernel, [field], [near_solved, (table, F32)],
-        part_two, local_two, *arrived, flux, neighbour_slot, orient, lifting, limit,
+        fifth_kernel, [field], [near_solved, pltpu.VMEM(table, F32)],
+        part_two, local_two, *arrived, flux, slot, orient, lifting, limit,
     )
     return jnp.transpose(updated, (1, 0, 2))
 

time: 51.1 us -> 60.4 us (1.18)
  the two profiles are of different devices: /device:TPU:26 before, /device:TPU:0 now
where the time goes in v1:
time: 60.4 us; the launch traced here: 59.9 us
  Pallas kernels  19.2 us (32%)
  blocking collectives  18.2 us (30%)
  starting transfers between devices  14 us (23%)
  local copies, waits for them, and re-layouts  8.13 us (13%)
    pallas_call x5, Pallas kernels, run(): pl.pallas_call(body, out_shape=[out if isinstance(out, jax.ShapeDtypeStru...  19.2 us
    all_to_all x2, blocking collectives, exchange(): lax.all_to_all(value, ('dom', 'sub'), 0, 0, axis_index_groups=blocks(shift))  18.2 us
    all_to_all x2, starting transfers between devices, exchange(): lax.all_to_all(value, ('dom', 'sub'), 0, 0, axis_index_groups=blocks(shift))  14 us
    unnamed x26, local copies, waits for them, and re-layouts  8.13 us
  transfers between devices with their start and end apart: 2, of which 1 were waited for; matrix products, arithmetic and copies ran while one was open for 0% of the time, Pallas kernels for 6%

profile of v1, /device:TPU:0, one launch (start us, length us, event | category | flops | bytes accessed | tf_op | source)
XLA Modules:
  0.0 59.9 jit_solution(16782727331662022330)
XLA Ops:
  0.0 7.4 %first_kernel.1 = (f32[9,56,128]{2,1,0:T(8,128)S(1)}, f32[3,56,56]{2,1,0:T(8,128)S(1)}, f32[21,4,56]{2,1,0:T(4,128)}, f32[9,9,3,128]{3,2,1,0:T(4,128)S(1)}, s32[...) custom-call(f32[9,56,128]{2,1,0:T(8,128)} %bitcast.9, ...), custom_call_target="tpu_custom_call" | custom-call | tf_op jit(solution)/shard_map/first_kernel/pallas_call | solution.py:442
  7.4 0.0 copy-start
  7.4 0.7 %copy-done = f32[9,56,128]{2,1,0:T(8,128)} copy-done((f32[9,56,128]{2,1,0:T(8,128)}, f32[9,56,128]{2,1,0:T(8,128)S(1)}, u32[]{:S(2)}) %copy-start) | copy-done | bytes 258072
  8.1 0.0 copy-start.9
  8.1 9.9 %all_to_all.20.from_even = f32[4,120,128]{2,1,0:T(8,128)S(1)} all-to-all(f32[4,120,128]{2,1,0:T(8,128)S(1)} %get-tuple-element.46), channel_id=1, replica_groups={{0,1,4,5},{2,3,6,7},{8,9,12,13},{10,11,14,15},{16,17,20,21},{18,19,22,2..., dimensions={0} | all-to-all | bytes 491520 | tf_op jit(solution)/shard_map/all_to_all | solution.py:469
  17.9 0.0 copy-done.9
  17.9 7.3 %all-to-all-start.1 = ((f32[4,120,128]{2,1,0:T(8,128)}), f32[4,120,128]{2,1,0:T(8,128)S(1)}, u32[]{:S(2)}, u32[]{:S(2)}) async-start(f32[4,120,128]{2,1,0:T(8,128)} %get-tuple-element.47), calls=%async_computation.1 | async-start | bytes 491520 | tf_op jit(solution)/shard_map/all_to_all | solution.py:469
  25.2 2.1 %second_kernel.1 = (f32[9,56,128]{2,1,0:T(8,128)S(1)}, f32[216,512]{1,0:T(8,128)S(1)}, f32[56,288]{1,0:T(8,128)S(1)}, f32[168,192]{1,0:T(8,128)S(1)}) custom-call(f32[9,56,128]{2,1,0:T(8,128)S(1)} %get-tuple-element.34.state, f32[9,56,128]{2,1,0:T(8,128)S(1)} %get-tuple-element.35.first, f32[216,512]{1,0:T(8,128)S(1)} %get-tuple-element.37.table.table_one, ...), custom_call_target="tpu_custom_call" | custom-call | tf_op jit(solution)/shard_map/second_kernel/pallas_call | solution.py:442
  27.3 0.0 copy-start.2
  27.3 0.7 %copy-done.2 = f32[9,56,128]{2,1,0:T(8,128)} copy-done((f32[9,56,128]{2,1,0:T(8,128)}, f32[9,56,128]{2,1,0:T(8,128)S(1)}, u32[]{:S(2)}) %copy-start.2) | copy-done | bytes 258072
  28.0 0.0 copy-start.11
  28.0 0.7 %copy-done.11 = f32[168,192]{1,0:T(8,128)} copy-done((f32[168,192]{1,0:T(8,128)}, f32[168,192]{1,0:T(8,128)S(1)}, u32[]{:S(2)}) %copy-start.11) | copy-done | bytes 129048
  28.7 0.0 all-to-all-done.1.from_odd
  28.7 0.0 copy-start.1
  28.7 0.9 %copy-done.1 = f32[9,56,128]{2,1,0:T(8,128)S(1)} copy-done((f32[9,56,128]{2,1,0:T(8,128)S(1)}, f32[9,56,128]{2,1,0:T(8,128)}, u32[]{:S(2)}) %copy-start.1) | copy-done | bytes 258072
  29.6 0.0 copy-start.3
  29.6 0.9 %copy-done.3 = f32[9,56,128]{2,1,0:T(8,128)S(1)} copy-done((f32[9,56,128]{2,1,0:T(8,128)S(1)}, f32[9,56,128]{2,1,0:T(8,128)}, u32[]{:S(2)}) %copy-start.3) | copy-done | bytes 258072
  30.6 0.0 copy-start.10
  30.6 0.9 %copy-done.10 = f32[168,192]{1,0:T(8,128)S(1)} copy-done((f32[168,192]{1,0:T(8,128)S(1)}, f32[168,192]{1,0:T(8,128)}, u32[]{:S(2)}) %copy-start.10) | copy-done | bytes 129048
  31.5 6.3 %third_kernel.1 = (f32[9,56,128]{2,1,0:T(8,128)S(1)}, f32[9,56,128]{2,1,0:T(8,128)S(1)}, f32[216,512]{1,0:T(8,128)S(1)}, f32[216,512]{1,0:T(8,128)S(1)}, f32[4,1...) custom-call(f32[9,56,128]{2,1,0:T(8,128)S(1)} %get-tuple-element.34.state, f32[9,56,128]{2,1,0:T(8,128)S(1)} %get-tuple-element.35.first, ...), custom_call_target="tpu_custom_call" | custom-call | tf_op jit(solution)/shard_map/third_kernel/pallas_call | solution.py:442
  37.8 0.0 copy-start.4
  37.8 0.7 %copy-done.4 = f32[9,56,128]{2,1,0:T(8,128)} copy-done((f32[9,56,128]{2,1,0:T(8,128)}, f32[9,56,128]{2,1,0:T(8,128)S(1)}, u32[]{:S(2)}) %copy-start.4) | copy-done | bytes 258072
  38.5 0.7 %copy-done.6 = f32[9,56,128]{2,1,0:T(8,128)} copy-done((f32[9,56,128]{2,1,0:T(8,128)}, f32[9,56,128]{2,1,0:T(8,128)S(1)}, u32[]{:S(2)}) %copy-start.6) | copy-done | bytes 258072
  39.2 8.3 %all_to_all.21.from_even = f32[4,120,128]{2,1,0:T(8,128)S(1)} all-to-all(f32[4,120,128]{2,1,0:T(8,128)S(1)} %get-tuple-element.60), channel_id=1, replica_groups={{0,1,4,5},{2,3,6,7},{8,9,12,13},{10,11,14,15},{16,17,20,21},{18,19,22,2..., dimensions={0} | all-to-all | bytes 491520 | tf_op jit(solution)/shard_map/all_to_all | solution.py:469
  47.5 0.0 copy-done.8
  47.5 6.7 %all-to-all-start.3 = ((f32[4,120,128]{2,1,0:T(8,128)}), f32[4,120,128]{2,1,0:T(8,128)S(1)}, u32[]{:S(2)}, u32[]{:S(2)}) async-start(f32[4,120,128]{2,1,0:T(8,128)} %copy-done.8), calls=%async_computation.3 | async-start | bytes 491520 | tf_op jit(solution)/shard_map/all_to_all | solution.py:469
  54.3 0.0 copy-done.5
  54.3 0.9 %copy-done.7 = f32[9,56,128]{2,1,0:T(8,128)S(1)} copy-done((f32[9,56,128]{2,1,0:T(8,128)S(1)}, f32[9,56,128]{2,1,0:T(8,128)}, u32[]{:S(2)}) %copy-start.7) | copy-done | bytes 258072
  55.2 0.9 %copy-done.12 = f32[168,192]{1,0:T(8,128)S(1)} copy-done((f32[168,192]{1,0:T(8,128)S(1)}, f32[168,192]{1,0:T(8,128)}, u32[]{:S(2)}) %copy-start.12) | copy-done | bytes 129048
  56.1 1.4 %fourth_kernel.1 = (f32[9,56,128]{2,1,0:T(8,128)S(1)}, f32[216,512]{1,0:T(8,128)S(1)}) custom-call(f32[9,56,128]{2,1,0:T(8,128)S(1)} %copy-done.5, f32[9,56,128]{2,1,0:T(8,128)S(1)} %copy-done.7, f32[216,512]{1,0:T(8,128)S(1)} %get-tuple-element.37.table.table_one, f32[216,512]{1,0:T(8,128)S(1)} %get-tuple-element.55.table_two, ...), custom_call_target="tpu_custom_call" | custom-call | tf_op jit(solution)/shard_map/fourth_kernel/pallas_call | solution.py:442
  57.6 0.4 all-to-all-done.3.from_odd
  57.9 2.0 %fifth_kernel.1 = f32[9,56,128]{2,1,0:T(8,128)} custom-call(f32[9,56,128]{2,1,0:T(8,128)S(1)} %get-tuple-element.58.part, f32[216,512]{1,0:T(8,128)S(1)} %get-tuple-element.59.picked_local, f32[4,120,128]{2,1,0:T(8,128)S(1)} %all_to_all.21.from_even, f32[4,120,128]{2,1,0:T(8,128)S(1)} %all-to-all-done.3.from_odd, ...), custom_call_target="tpu_custom_call" | custom-call | tf_op jit(solution)/shard_map/fifth_kernel/pallas_call | solution.py:442
  (5 shorter events, 0.0 us)
Async XLA Ops:
  7.4 0.7 %copy-start = (f32[9,56,128]{2,1,0:T(8,128)}, f32[9,56,128]{2,1,0:T(8,128)S(1)}, u32[]{:S(2)}) copy-start(f32[9,56,128]{2,1,0:T(8,128)S(1)} %get-tuple-element.36.second) | copy-start | bytes 774148
  8.1 9.9 %copy-start.9 = (f32[168,192]{1,0:T(8,128)}, f32[168,192]{1,0:T(8,128)S(1)}, u32[]{:S(2)}) copy-start(f32[168,192]{1,0:T(8,128)S(1)} %get-tuple-element.48.stiff_fold) | copy-start | bytes 387076
  17.9 10.8 %all-to-all-start.1 = ((f32[4,120,128]{2,1,0:T(8,128)}), f32[4,120,128]{2,1,0:T(8,128)S(1)}, u32[]{:S(2)}, u32[]{:S(2)}) async-start(f32[4,120,128]{2,1,0:T(8,128)} %get-tuple-element.47), calls=%async_computation.1 | async-start | bytes 491520 | tf_op jit(solution)/shard_map/all_to_all | solution.py:469
  27.3 0.7 %copy-start.2 = (f32[9,56,128]{2,1,0:T(8,128)}, f32[9,56,128]{2,1,0:T(8,128)S(1)}, u32[]{:S(2)}) copy-start(f32[9,56,128]{2,1,0:T(8,128)S(1)} %get-tuple-element.44.part) | copy-start | bytes 774148
  28.0 0.7 %copy-start.11 = (f32[168,192]{1,0:T(8,128)}, f32[168,192]{1,0:T(8,128)S(1)}, u32[]{:S(2)}) copy-start(f32[168,192]{1,0:T(8,128)S(1)} %get-tuple-element.57.turned_fold) | copy-start | bytes 387076
  28.7 0.9 %copy-start.1 = (f32[9,56,128]{2,1,0:T(8,128)S(1)}, f32[9,56,128]{2,1,0:T(8,128)}, u32[]{:S(2)}) copy-start(f32[9,56,128]{2,1,0:T(8,128)} %copy-done) | copy-start | bytes 774148
  29.6 0.9 %copy-start.3 = (f32[9,56,128]{2,1,0:T(8,128)S(1)}, f32[9,56,128]{2,1,0:T(8,128)}, u32[]{:S(2)}) copy-start(f32[9,56,128]{2,1,0:T(8,128)} %copy-done.2) | copy-start | bytes 774148
  30.6 0.9 %copy-start.10 = (f32[168,192]{1,0:T(8,128)S(1)}, f32[168,192]{1,0:T(8,128)}, u32[]{:S(2)}) copy-start(f32[168,192]{1,0:T(8,128)} %copy-done.9) | copy-start | bytes 387076
  37.8 0.7 %copy-start.4 = (f32[9,56,128]{2,1,0:T(8,128)}, f32[9,56,128]{2,1,0:T(8,128)S(1)}, u32[]{:S(2)}) copy-start(f32[9,56,128]{2,1,0:T(8,128)S(1)} %get-tuple-element.53.middle) | copy-start | bytes 774148
  38.5 0.7 %copy-start.6 = (f32[9,56,128]{2,1,0:T(8,128)}, f32[9,56,128]{2,1,0:T(8,128)S(1)}, u32[]{:S(2)}) copy-start(f32[9,56,128]{2,1,0:T(8,128)S(1)} %get-tuple-element.54.integral) | copy-start | bytes 774148
  39.2 8.3 %copy-start.8 = (f32[4,120,128]{2,1,0:T(8,128)}, f32[4,120,128]{2,1,0:T(8,128)S(1)}, u32[]{:S(2)}) copy-start(f32[4,120,128]{2,1,0:T(8,128)S(1)} %get-tuple-element.61) | copy-start | bytes 737284
  47.5 6.7 %copy-start.5 = (f32[9,56,128]{2,1,0:T(8,128)S(1)}, f32[9,56,128]{2,1,0:T(8,128)}, u32[]{:S(2)}) copy-start(f32[9,56,128]{2,1,0:T(8,128)} %copy-done.4) | copy-start | bytes 774148
  47.5 10.4 %all-to-all-start.3 = ((f32[4,120,128]{2,1,0:T(8,128)}), f32[4,120,128]{2,1,0:T(8,128)S(1)}, u32[]{:S(2)}, u32[]{:S(2)}) async-start(f32[4,120,128]{2,1,0:T(8,128)} %copy-done.8), calls=%async_computation.3 | async-start | bytes 491520 | tf_op jit(solution)/shard_map/all_to_all | solution.py:469
  54.3 0.9 %copy-start.7 = (f32[9,56,128]{2,1,0:T(8,128)S(1)}, f32[9,56,128]{2,1,0:T(8,128)}, u32[]{:S(2)}) copy-start(f32[9,56,128]{2,1,0:T(8,128)} %copy-done.6) | copy-start | bytes 774148
  55.2 0.9 %copy-start.12 = (f32[168,192]{1,0:T(8,128)S(1)}, f32[168,192]{1,0:T(8,128)}, u32[]{:S(2)}) copy-start(f32[168,192]{1,0:T(8,128)} %copy-done.11) | copy-start | bytes 387076

commit v2 on v1

--- a/solution.py
+++ b/solution.py
@@ -1,3 +1,5 @@
+import math
+
 import jax
 import jax.numpy as jnp
 from jax import lax
@@ -17,8 +19,8 @@
 
 DOM_GROUPS = ((0, 5), (5, 4))
 SUB_GROUPS = ((0, 3), (3, 2), (5, 2), (7, 2))
-
-GRANT = 32
+PACKING = (DOM_GROUPS, DOM_GROUPS, SUB_GROUPS, SUB_GROUPS)
+
 INPUTS = 11
 FIRST_USED = 5
 
@@ -68,7 +70,12 @@
     return (dot(high, outer) + dot(low, inner)).astype(BF16)
 
 
-def mix_jacobians(stiffened, jac, basis, quants, lanes, write):
+def stiffen(stiff_fold, values, target, start, lanes):
+    folded = jnp.concatenate([fold_rows(value) for value in values], axis=1)
+    target[:, start * lanes:(start + len(values)) * lanes] = dot(stiff_fold, folded)
+
+
+def mix_jacobians(stiffened, jac, basis, quants, lanes, take):
     for start in range(0, quants, GROUP):
         totals = [None] * GROUP
         for q in range(quants):
@@ -77,8 +84,7 @@
                 for i in range(GROUP):
                     term = block * jac[q, start + i, d:d + 1, :]
                     totals[i] = term if totals[i] is None else totals[i] + term
-        for i in range(GROUP):
-            write(start + i, totals[i])
+        take(start, totals)
 
 
 def mix_faces(table, flux, side, quants, lanes, write):
@@ -101,74 +107,56 @@
             padded[f * ROWS + m:f * ROWS + m + 1, 0:basis] = projector[m, f:f + 1, :]
 
 
-def predict(stiff_fold, jac, folded, stiffened, first, second, basis, quants, lanes):
-    def step(_, scales):
-        factor, power, number = scales
-        stiffened[...] = dot(stiff_fold, folded[...])
-
-        def write(p, total):
-            folded[:, p * lanes:(p + 1) * lanes] = fold_rows(total)
-            first[p] = first[p] + factor * total
-            if second is not None:
-                second[p] = second[p] + (factor * (power - 1.0)) * total
-
-        mix_jacobians(stiffened, jac, basis, quants, lanes, write)
-        return factor / (number + 1.0), power * 2.0, number + 1.0
-
-    lax.fori_loop(0, ORDER - 1, step, (jnp.float32(0.5), jnp.float32(4.0), jnp.float32(2.0)))
-
-
-def project_table(padded, folded, table, basis, quants, lanes):
-    flat = dot(fold_columns(padded[:, 0:basis]), folded[...])
-    for q in range(quants):
-        for f in range(4):
-            table[q * ROWS:(q + 1) * ROWS, f * lanes:(f + 1) * lanes] = flat[
-                f * ROWS:(f + 1) * ROWS, q * lanes:(q + 1) * lanes
-            ]
-
-
-def grid_spot():
-    i, j = lax.axis_index("dom"), lax.axis_index("sub")
-    return (
-        lax.rem(i, 2), lax.rem(j, 2),
-        i > 0, i < lax.axis_size("dom") - 1, j > 0, j < lax.axis_size("sub") - 1,
-    )
-
-
-def partners(parity_dom, parity_sub, tiling):
-    u = parity_dom if tiling == 0 else 1 - parity_dom
-    v = parity_sub if tiling == 0 else 1 - parity_sub
-    return (1 - u) * 2 + v, u * 2 + (1 - v)
+def predict(stiff_fold, jac, state, stiffened, first, second, basis, quants, lanes):
+    for start in range(0, quants, GROUP):
+        values = [state(q) for q in range(start, start + GROUP)]
+        stiffen(stiff_fold, values, stiffened.at[0], start, lanes)
+    for order in range(1, ORDER):
+        factor = 1.0 / math.factorial(order + 1)
+
+        def take(start, totals):
+            if order + 1 < ORDER:
+                stiffen(stiff_fold, totals, stiffened.at[order % 2], start, lanes)
+            for p, total in enumerate(totals, start):
+                first[p] = first[p] + factor * total
+                if second is not None:
+                    second[p] = second[p] + (2.0 ** (order + 1) - 1.0) * factor * total
+
+        mix_jacobians(stiffened.at[(order - 1) % 2], jac, basis, quants, lanes, take)
+
+
+def project_table(padded, field, table, basis, quants, lanes):
+    fold = fold_columns(padded[:, 0:basis])
+    for start in range(0, quants, GROUP):
+        values = [fold_rows(field(q)) for q in range(start, start + GROUP)]
+        flat = dot(fold, jnp.concatenate(values, axis=1))
+        for q in range(start, start + GROUP):
+            for f in range(4):
+                table[q * ROWS:(q + 1) * ROWS, f * lanes:(f + 1) * lanes] = flat[
+                    f * ROWS:(f + 1) * ROWS, (q - start) * lanes:(q - start + 1) * lanes
+                ]
 
 
 def pick_sends(table, send_row, outs, lanes):
     faces = table.shape[1]
-    parity_dom, parity_sub, *_ = grid_spot()
     low = jnp.broadcast_to(send_row[:, 0:lanes], (8, lanes))
     lane = iota((8, lanes), 1)
     turned = pltpu.roll(low, SLOTS_DOM, 1)
-    to_lower = jnp.where(lane < SLOTS_DOM, low, turned)
-    to_upper = jnp.where(lane < SLOTS_DOM, turned, low)
     high = send_row[:, 2 * SLOTS_DOM:2 * SLOTS_DOM + 2 * SLOTS_SUB]
     spread = jnp.broadcast_to(jnp.concatenate([high, high], axis=1), (8, lanes))
     moved = pltpu.roll(spread, SLOTS_SUB, 1)
     left = lax.rem(lane, 2 * SLOTS_SUB) < SLOTS_SUB
-    to_left = jnp.where(left, spread, moved)
-    to_right = jnp.where(left, moved, spread)
-    even_dom, even_sub = parity_dom == 0, parity_sub == 0
     pieces = [
-        jnp.where(even_dom, to_upper, to_lower),
-        jnp.where(even_dom, to_lower, to_upper),
-        jnp.where(even_sub, to_right, to_left),
-        jnp.where(even_sub, to_left, to_right),
+        jnp.where(lane < SLOTS_DOM, low, turned),
+        jnp.where(lane < SLOTS_DOM, turned, low),
+        jnp.where(left, spread, moved),
+        jnp.where(left, moved, spread),
     ]
     index = jnp.concatenate([piece[0:1] for piece in pieces], axis=1)
     chosen = one_hot(index, 0, faces)
     upper, lower = halves(table[...])
     sent = dot(upper, chosen) + dot(lower, chosen)
-    for k, groups in enumerate((DOM_GROUPS, DOM_GROUPS, SUB_GROUPS, SUB_GROUPS)):
-        out = outs[k % 2]
-        place = partners(parity_dom, parity_sub, k % 2)[k // 2]
+    for k, (out, groups) in enumerate(zip(outs, PACKING)):
         width = lanes // len(groups)
         values = sent[:, k * lanes:(k + 1) * lanes]
         start, count = groups[0]
@@ -181,16 +169,16 @@
                 head = jnp.where(
                     spot >= g * width, values[start * ROWS:start * ROWS + least], head
                 )
-        out[place, 0:least] = head
-        out[place, least:count * ROWS] = packed[least:]
-
-
-def spread_received(arrived, valid, groups, lanes):
+        out[0:least] = head
+        out[least:count * ROWS] = packed[least:]
+
+
+def spread_received(arrived, groups, lanes):
     width = lanes // len(groups)
     parts = []
     for g, (_, count) in enumerate(groups):
         place = iota((count * ROWS, lanes), 1)
-        mine = (place >= g * width) & (place < (g + 1) * width) & valid
+        mine = (place >= g * width) & (place < (g + 1) * width)
         parts.append(jnp.where(mine, arrived[0:count * ROWS], 0.0))
     return jnp.concatenate(parts, axis=0)
 
@@ -202,39 +190,18 @@
 
 
 def pick_received(arrived, slot, faces, lanes):
-    parity_dom, parity_sub, lower, upper, left, right = grid_spot()
-    even_dom, even_sub = parity_dom == 0, parity_sub == 0
+    spread = jnp.concatenate(
+        [spread_received(item[...], groups, lanes) for item, groups in zip(arrived, PACKING)],
+        axis=1,
+    )
     starts = (faces, faces + SLOTS_DOM, faces + 2 * SLOTS_DOM, faces + 2 * SLOTS_DOM + SLOTS_SUB)
-    true = parity_dom >= 0
-    firsts = (
-        jnp.where(even_dom, starts[1], starts[0]), jnp.where(even_dom, starts[0], starts[1]),
-        jnp.where(even_sub, starts[3], starts[2]), jnp.where(even_sub, starts[2], starts[3]),
-    )
-    valid = (
-        true, (even_dom & lower) | (~even_dom & upper),
-        true, (even_sub & left) | (~even_sub & right),
-    )
     widths = (SLOTS_DOM, SLOTS_DOM, SLOTS_SUB, SLOTS_SUB)
-    all_groups = (DOM_GROUPS, DOM_GROUPS, SUB_GROUPS, SUB_GROUPS)
-    spread = jnp.concatenate(
-        [
-            spread_received(
-                arrived[k % 2][
-                    partners(parity_dom, parity_sub, k % 2)[k // 2],
-                    0:groups[0][1] * ROWS,
-                ],
-                valid[k], groups, lanes,
-            )
-            for k, groups in enumerate(all_groups)
-        ],
-        axis=1,
-    )
     chosen = jnp.concatenate(
         [
             jnp.concatenate(
                 [one_hot(slot[f:f + 1], first, lanes, width) for f in range(4)], axis=1
             )
-            for first, width in zip(firsts, widths)
+            for first, width in zip(starts, widths)
         ],
         axis=0,
     )
@@ -248,12 +215,12 @@
 
 
 def local_update(
-    base, integral, table, jac, turned_fold, flux, lifting, folded, stiffened, solved, write,
+    base, integral, table, jac, turned_fold, flux, lifting, stiffened, solved, write,
     basis, quants, lanes,
 ):
-    for q in range(quants):
-        folded[:, q * lanes:(q + 1) * lanes] = fold_rows(integral(q))
-    stiffened[...] = dot(turned_fold, folded[...])
+    for start in range(0, quants, GROUP):
+        values = [integral(q) for q in range(start, start + GROUP)]
+        stiffen(turned_fold, values, stiffened, start, lanes)
 
     def keep(f, p, total):
         solved[f * ROWS:(f + 1) * ROWS, p * lanes:(p + 1) * lanes] = total
@@ -261,10 +228,12 @@
     mix_faces(table, flux, 0, quants, lanes, keep)
     high, low = halves(solved[...])
     own = lift(lifting, high, low)
-    mix_jacobians(
-        stiffened, jac, basis, quants, lanes,
-        lambda p, total: write(p, base(p) + total - own[:, p * lanes:(p + 1) * lanes]),
-    )
+
+    def take(start, totals):
+        for p, total in enumerate(totals, start):
+            write(p, base(p) + total - own[:, p * lanes:(p + 1) * lanes])
+
+    mix_jacobians(stiffened, jac, basis, quants, lanes, take)
 
 
 def near_lift(picked, flux, orient, lifting, solved, quants, lanes):
@@ -303,8 +272,7 @@
 def first_kernel(*refs):
     inputs, refs = refs[:INPUTS], refs[INPUTS:]
     held, refs = refs[:INPUTS], refs[INPUTS:]
-    (first, second, table, padded, stiff_fold, send_even, send_odd,
-     folded, stiffened, arrivals) = refs
+    first, second, table, padded, stiff_fold, *sends, stiffened, arrivals = refs
     copies = [
         pltpu.make_async_copy(source, target, arrivals.at[k])
         for k, (source, target) in enumerate(zip(inputs, held))
@@ -319,16 +287,15 @@
         value = state[q]
         first[q] = value
         second[q] = value
-        folded[:, q * lanes:(q + 1) * lanes] = fold_rows(value)
     fill_projector(projector, padded)
     stacked = jnp.concatenate([stiffness[d] for d in range(3)], axis=0)
     fold = fold_columns(stacked)
     stiff_fold[...] = fold.astype(F32)
-    predict(fold, jac, folded, stiffened, first, second, basis, quants, lanes)
-    for q in range(quants):
-        folded[:, q * lanes:(q + 1) * lanes] = fold_rows(first[q])
-    project_table(padded, folded, table, basis, quants, lanes)
-    pick_sends(table, send_row, (send_even, send_odd), lanes)
+    predict(
+        fold, jac, lambda q: state[q], stiffened, first, second, basis, quants, lanes
+    )
+    project_table(padded, lambda q: first[q], table, basis, quants, lanes)
+    pick_sends(table, send_row, sends, lanes)
     for copy in copies[FIRST_USED:]:
         copy.wait()
 
@@ -336,7 +303,7 @@
 def second_kernel(
     state, first, table, jac, stiffness, padded, rotations, flux, slot,
     part, picked, lifting, turned_fold,
-    folded, stiffened, solved,
+    stiffened, solved,
 ):
     quants, basis, lanes = state.shape
     turned = jnp.concatenate([stiffness[d].T for d in range(3)], axis=0)
@@ -351,19 +318,19 @@
 
     local_update(
         lambda p: state[p], lambda q: first[q], table, jac, fold, flux, own_lifting,
-        folded, stiffened, solved, write, basis, quants, lanes,
+        stiffened, solved, write, basis, quants, lanes,
     )
 
 
 def third_kernel(
-    state, first, second, part, picked_local, from_even, from_odd,
+    state, first, second, part, picked_local, from_lower, from_upper, from_left, from_right,
     jac, stiff_fold, padded, flux, slot, orient, cluster, lifting, send_row,
-    middle, integral, picked, table, send_even, send_odd,
-    folded, stiffened, solved,
+    middle, integral, picked, table, to_lower, to_upper, to_left, to_right,
+    stiffened, solved,
 ):
     quants, basis, lanes = state.shape
     picked[...] = picked_local[...] + pick_received(
-        (from_even, from_odd), slot, 4 * lanes, lanes
+        (from_lower, from_upper, from_left, from_right), slot, 4 * lanes, lanes
     )
     near = near_lift(picked, flux, orient, lifting[...], solved, quants, lanes)
     fine = cluster[...] == 0
@@ -371,25 +338,23 @@
         value = jnp.where(fine, part[q] - near[:, q * lanes:(q + 1) * lanes], state[q])
         middle[q] = value
         integral[q] = value
-        folded[:, q * lanes:(q + 1) * lanes] = fold_rows(value)
     predict(
-        stiff_fold[...].astype(BF16), jac, folded, stiffened, integral, None,
+        stiff_fold[...].astype(BF16), jac, lambda q: middle[q], stiffened, integral, None,
         basis, quants, lanes,
     )
+    project_table(
+        padded, lambda q: jnp.where(fine, integral[q], second[q]), table, basis, quants, lanes
+    )
     for q in range(quants):
-        fine_first = integral[q]
-        late = jnp.where(fine, fine_first, second[q])
-        folded[:, q * lanes:(q + 1) * lanes] = fold_rows(late)
-        integral[q] = jnp.where(fine, fine_first, first[q] + second[q])
-    project_table(padded, folded, table, basis, quants, lanes)
-    pick_sends(table, send_row, (send_even, send_odd), lanes)
+        integral[q] = jnp.where(fine, integral[q], first[q] + second[q])
+    pick_sends(table, send_row, (to_lower, to_upper, to_left, to_right), lanes)
 
 
 def fourth_kernel(
     middle, integral, table_one, table_two, picked_one, jac, turned_fold, padded, flux, slot,
     cluster,
     part, picked,
-    folded, stiffened, solved, total_table,
+    stiffened, solved, total_table,
 ):
     quants, basis, lanes = middle.shape
     own_lifting = padded[...].T[0:basis]
@@ -404,19 +369,19 @@
 
     local_update(
         lambda p: middle[p], lambda q: integral[q], total_table, jac, turned_fold[...].astype(BF16), flux,
-        own_lifting, folded, stiffened, solved, write, basis, quants, lanes,
+        own_lifting, stiffened, solved, write, basis, quants, lanes,
     )
 
 
 def fifth_kernel(
-    part, picked_local, from_even, from_odd, flux, slot, orient, lifting,
+    part, picked_local, from_lower, from_upper, from_left, from_right, flux, slot, orient, lifting,
     yield_stress,
     updated,
     solved, picked,
 ):
     quants, basis, lanes = part.shape
     picked[...] = picked_local[...] + pick_received(
-        (from_even, from_odd), slot, 4 * lanes, lanes
+        (from_lower, from_upper, from_left, from_right), slot, 4 * lanes, lanes
     )
     near = near_lift(picked, flux, orient, lifting[...], solved, quants, lanes)
     stepped = [part[q] - near[:, q * lanes:(q + 1) * lanes] for q in range(quants)]
@@ -437,7 +402,7 @@
         updated[q] = stepped[q]
 
 
-def run(body, outs, scratch, *operands, space=pltpu.VMEM, grant=32):
+def run(body, outs, scratch, *operands, space=pltpu.VMEM):
     vmem = pl.BlockSpec(memory_space=pltpu.VMEM)
     return pl.pallas_call(
         body,
@@ -448,27 +413,25 @@
         in_specs=[pl.BlockSpec(memory_space=space)] * len(operands),
         out_specs=[vmem] * len(outs),
         scratch_shapes=scratch,
-        compiler_params=pltpu.CompilerParams(vmem_limit_bytes=grant * 1024 * 1024),
+        compiler_params=pltpu.CompilerParams(vmem_limit_bytes=32 * 1024 * 1024),
         name=body.__name__,
     )(*operands)
 
 
-def blocks(shift):
-    rows, columns = lax.axis_size("dom"), lax.axis_size("sub")
-    groups = []
-    for i in range(shift, rows + shift, 2):
-        for j in range(shift, columns + shift, 2):
-            groups.append(
-                [(i + u) % rows * columns + (j + v) % columns for u in (0, 1) for v in (0, 1)]
-            )
-    return groups
-
-
 def exchange(sends):
-    return [
-        lax.all_to_all(value, ("dom", "sub"), 0, 0, axis_index_groups=blocks(shift))
-        for shift, value in enumerate(sends)
-    ]
+    to_lower, to_upper, to_left, to_right = sends
+
+    def shift(value, axis, step):
+        size = lax.axis_size(axis)
+        pairs = [(i, i + step) for i in range(size) if 0 <= i + step < size]
+        return lax.ppermute(value, axis, pairs)
+
+    return (
+        shift(to_upper, "dom", 1),
+        shift(to_lower, "dom", -1),
+        shift(to_right, "sub", 1),
+        shift(to_left, "sub", -1),
+    )
 
 
 def on_device(
@@ -503,39 +466,39 @@
 
     field = (quants, basis, lanes)
     table = (quants * ROWS, 4 * lanes)
-    message = (4, DOM_GROUPS[0][1] * ROWS, lanes)
+    messages = [(groups[0][1] * ROWS, lanes) for groups in PACKING]
     depth = fold_depth(basis)
     flat = quants * lanes
     fold = (3 * basis, depth)
-    folded = pltpu.VMEM((depth, flat), BF16)
     stiffened = pltpu.VMEM((3 * basis, flat), F32)
+    two_stiffened = pltpu.VMEM((2, 3 * basis, flat), F32)
     own_solved = pltpu.VMEM((4 * ROWS, flat), F32)
     near_solved = pltpu.VMEM((2 * 3 * 4 * ROWS, flat), F32)
 
     outs = run(
         first_kernel,
-        held + [field, field, table, (4 * ROWS, 128), fold, message, message],
-        [folded, stiffened, pltpu.SemaphoreType.DMA((INPUTS,))],
-        *inputs, space=pl.ANY, grant=GRANT,
+        held + [field, field, table, (4 * ROWS, 128), fold] + messages,
+        [two_stiffened, pltpu.SemaphoreType.DMA((INPUTS,))],
+        *inputs, space=pl.ANY,
     )
     state, stiff, _, jac, send_row, flux, turns, slot, orient, cluster, limit = outs[:INPUTS]
     first, second, table_one, padded, stiff_fold, *sends = outs[INPUTS:]
     arrived = exchange(sends)
     part_one, local_one, lifting, turned_fold = run(
         second_kernel, [field, table, (basis, 3 * 4 * ROWS), fold],
-        [folded, stiffened, own_solved],
+        [stiffened, own_solved],
         state, first, table_one, jac, stiff, padded, turns, flux, slot,
     )
     middle, integral, picked_one, table_two, *sends = run(
-        third_kernel, [field, field, table, table, message, message],
-        [folded, stiffened, near_solved],
+        third_kernel, [field, field, table, table] + messages,
+        [two_stiffened, near_solved],
         state, first, second, part_one, local_one, *arrived,
         jac, stiff_fold, padded, flux, slot, orient, cluster, lifting, send_row,
     )
     arrived = exchange(sends)
     part_two, local_two = run(
         fourth_kernel, [field, table],
-        [folded, stiffened, own_solved, pltpu.VMEM(table, F32)],
+        [stiffened, own_solved, pltpu.VMEM(table, F32)],
         middle, integral, table_one, table_two, picked_one, jac, turned_fold, padded, flux,
         slot, cluster,
     )

time: 60.4 us -> 44.6 us (0.74)
  the two profiles are of different devices: /device:TPU:0 before, /device:TPU:8 now
where the time goes in v2:
time: 44.6 us; the launch traced here: 44.3 us
  starting transfers between devices  21.4 us (48%)
  Pallas kernels  17.3 us (39%)
  waiting for transfers between devices  5.42 us (12%)
    ppermute x8, starting transfers between devices, shift(): return lax.ppermute(value, axis, pairs)  21.4 us
    pallas_call x5, Pallas kernels, run(): pl.pallas_call(body, out_shape=[out if isinstance(out, jax.ShapeDtypeStru...  17.3 us
    ppermute x8, waiting for transfers between devices, shift(): return lax.ppermute(value, axis, pairs)  5.42 us
  transfers between devices with their start and end apart: 8, of which 2 were waited for; matrix products, arithmetic and copies ran while one was open for 0% of the time, Pallas kernels for 8%

profile of v2, /device:TPU:8, one launch (start us, length us, event | category | flops | bytes accessed | tf_op | source)
XLA Modules:
  0.0 44.3 jit_solution(16446698703870167182)
XLA Ops:
  0.0 6.3 %first_kernel.1 = (f32[9,56,128]{2,1,0:T(8,128)S(1)}, f32[3,56,56]{2,1,0:T(8,128)S(1)}, f32[21,4,56]{2,1,0:T(4,128)}, f32[9,9,3,128]{3,2,1,0:T(4,128)S(1)}, s32[...) custom-call(f32[9,56,128]{2,1,0:T(8,128)} %bitcast.9, ...), custom_call_target="tpu_custom_call" | custom-call | tf_op jit(solution)/shard_map/first_kernel/pallas_call | solution.py:407
  6.3 1.9 %collective-permute-start = (f32[120,128]{1,0:T(8,128)S(1)}, f32[120,128]{1,0:T(8,128)S(1)}, u32[]{:S(2)}, u32[]{:S(2)}) collective-permute-start(f32[120,128]{1,0:T(8,128)S(1)} %get-tuple-element.50), channel_id=1, source_target_pairs={{0,4},{4,8},{8,12},{12,16},{16,20},{20,24},{24,28},{1,5},{5,9},{9,... | collective-permute-start | bytes 184328 | tf_op jit(solution)/shard_map/ppermute | solution.py:427
  8.2 3.6 %collective-permute-start.1 = (f32[120,128]{1,0:T(8,128)S(1)}, f32[120,128]{1,0:T(8,128)S(1)}, u32[]{:S(2)}, u32[]{:S(2)}) collective-permute-start(f32[120,128]{1,0:T(8,128)S(1)} %get-tuple-element.51), channel_id=1, source_target_pairs={{4,0},{8,4},{12,8},{16,12},{20,16},{24,20},{28,24},{5,1},{9,5},{13... | collective-permute-start | bytes 184328 | tf_op jit(solution)/shard_map/ppermute | solution.py:427
  11.9 3.4 %collective-permute-start.2 = (f32[72,128]{1,0:T(8,128)S(1)}, f32[72,128]{1,0:T(8,128)S(1)}, u32[]{:S(2)}, u32[]{:S(2)}) collective-permute-start(f32[72,128]{1,0:T(8,128)S(1)} %get-tuple-element.52), channel_id=1, source_target_pairs={{0,1},{1,2},{2,3},{4,5},{5,6},{6,7},{8,9},{9,10},{10,11},{12,13},{... | collective-permute-start | bytes 110600 | tf_op jit(solution)/shard_map/ppermute | solution.py:427
  15.3 1.3 %collective-permute-start.3 = (f32[72,128]{1,0:T(8,128)S(1)}, f32[72,128]{1,0:T(8,128)S(1)}, u32[]{:S(2)}, u32[]{:S(2)}) collective-permute-start(f32[72,128]{1,0:T(8,128)S(1)} %get-tuple-element.53), channel_id=1, source_target_pairs={{1,0},{2,1},{3,2},{5,4},{6,5},{7,6},{9,8},{10,9},{11,10},{13,12},{... | collective-permute-start | bytes 110600 | tf_op jit(solution)/shard_map/ppermute | solution.py:427
  16.6 2.1 %second_kernel.1 = (f32[9,56,128]{2,1,0:T(8,128)S(1)}, f32[216,512]{1,0:T(8,128)S(1)}, f32[56,288]{1,0:T(8,128)S(1)}, f32[168,192]{1,0:T(8,128)S(1)}) custom-call(f32[9,56,128]{2,1,0:T(8,128)S(1)} %get-tuple-element.38.state, f32[9,56,128]{2,1,0:T(8,128)S(1)} %get-tuple-element.39.first, f32[216,512]{1,0:T(8,128)S(1)} %get-tuple-element.41.table.table_one, ...), custom_call_target="tpu_custom_call" | custom-call | tf_op jit(solution)/shard_map/second_kernel/pallas_call | solution.py:407
  18.7 0.0 collective-permute-done.2.from_left
  18.7 2.4 %collective-permute-done.3.from_right = f32[72,128]{1,0:T(8,128)S(1)} collective-permute-done((f32[72,128]{1,0:T(8,128)S(1)}, f32[72,128]{1,0:T(8,128)S(1)}, u32[]{:S(2)}, u32[]{:S(2)}) %collective-permute-start.3) | collective-permute-done | bytes 36896 | tf_op jit(solution)/shard_map/ppermute | solution.py:427
  21.1 0.0 collective-permute-done.from_lower
  21.1 0.0 collective-permute-done.1.from_upper
  21.1 5.4 %third_kernel.1 = (f32[9,56,128]{2,1,0:T(8,128)S(1)}, f32[9,56,128]{2,1,0:T(8,128)S(1)}, f32[216,512]{1,0:T(8,128)S(1)}, f32[216,512]{1,0:T(8,128)S(1)}, f32[120...) custom-call(f32[9,56,128]{2,1,0:T(8,128)S(1)} %get-tuple-element.38.state, ...), custom_call_target="tpu_custom_call" | custom-call | tf_op jit(solution)/shard_map/third_kernel/pallas_call | solution.py:407
  26.5 1.9 %collective-permute-start.4 = (f32[120,128]{1,0:T(8,128)S(1)}, f32[120,128]{1,0:T(8,128)S(1)}, u32[]{:S(2)}, u32[]{:S(2)}) collective-permute-start(f32[120,128]{1,0:T(8,128)S(1)} %get-tuple-element.66), channel_id=1, source_target_pairs={{0,4},{4,8},{8,12},{12,16},{16,20},{20,24},{24,28},{1,5},{5,9},{9,... | collective-permute-start | bytes 184328 | tf_op jit(solution)/shard_map/ppermute | solution.py:427
  28.4 3.6 %collective-permute-start.5 = (f32[120,128]{1,0:T(8,128)S(1)}, f32[120,128]{1,0:T(8,128)S(1)}, u32[]{:S(2)}, u32[]{:S(2)}) collective-permute-start(f32[120,128]{1,0:T(8,128)S(1)} %get-tuple-element.67), channel_id=1, source_target_pairs={{4,0},{8,4},{12,8},{16,12},{20,16},{24,20},{28,24},{5,1},{9,5},{13... | collective-permute-start | bytes 184328 | tf_op jit(solution)/shard_map/ppermute | solution.py:427
  32.1 4.3 %collective-permute-start.6 = (f32[72,128]{1,0:T(8,128)S(1)}, f32[72,128]{1,0:T(8,128)S(1)}, u32[]{:S(2)}, u32[]{:S(2)}) collective-permute-start(f32[72,128]{1,0:T(8,128)S(1)} %get-tuple-element.68), channel_id=1, source_target_pairs={{0,1},{1,2},{2,3},{4,5},{5,6},{6,7},{8,9},{9,10},{10,11},{12,13},{... | collective-permute-start | bytes 110600 | tf_op jit(solution)/shard_map/ppermute | solution.py:427
  36.4 1.3 %collective-permute-start.7 = (f32[72,128]{1,0:T(8,128)S(1)}, f32[72,128]{1,0:T(8,128)S(1)}, u32[]{:S(2)}, u32[]{:S(2)}) collective-permute-start(f32[72,128]{1,0:T(8,128)S(1)} %get-tuple-element.69), channel_id=1, source_target_pairs={{1,0},{2,1},{3,2},{5,4},{6,5},{7,6},{9,8},{10,9},{11,10},{13,12},{... | collective-permute-start | bytes 110600 | tf_op jit(solution)/shard_map/ppermute | solution.py:427
  37.7 1.5 %fourth_kernel.1 = (f32[9,56,128]{2,1,0:T(8,128)S(1)}, f32[216,512]{1,0:T(8,128)S(1)}) custom-call(f32[9,56,128]{2,1,0:T(8,128)S(1)} %get-tuple-element.59.middle, f32[9,56,128]{2,1,0:T(8,128)S(1)} %get-tuple-element.60.integral, f32[216,512]{1,0:T(8,128)S(1)} %get-tuple-element.41.table.table_one, f32[216,512]{1,0:T(8,128)S(1)} %get-tuple-element.61.table_two, ...), custom_call_target="tpu_custom_call" | custom-call | tf_op jit(solution)/shard_map/fourth_kernel/pallas_call | solution.py:407
  39.3 0.0 collective-permute-done.6.from_left
  39.3 3.0 %collective-permute-done.7.from_right = f32[72,128]{1,0:T(8,128)S(1)} collective-permute-done((f32[72,128]{1,0:T(8,128)S(1)}, f32[72,128]{1,0:T(8,128)S(1)}, u32[]{:S(2)}, u32[]{:S(2)}) %collective-permute-start.7) | collective-permute-done | bytes 36896 | tf_op jit(solution)/shard_map/ppermute | solution.py:427
  42.3 0.0 collective-permute-done.4.from_lower
  42.3 0.0 collective-permute-done.5.from_upper
  42.3 2.0 %fifth_kernel.1 = f32[9,56,128]{2,1,0:T(8,128)} custom-call(f32[9,56,128]{2,1,0:T(8,128)S(1)} %get-tuple-element.64.part, f32[216,512]{1,0:T(8,128)S(1)} %get-tuple-element.65.picked_local, f32[120,128]{1,0:T(8,128)S(1)} %collective-permute-done.4.from_lower, f32[120,128]{1,0:T(8,128)S(1)} %collective-permute-done.5.from_upper, ...), custom_call_target="tpu_custom_call" | custom-call | tf_op jit(solution)/shard_map/fifth_kernel/pallas_call | solution.py:407
Async XLA Ops:
  6.3 14.8 %collective-permute-start = (f32[120,128]{1,0:T(8,128)S(1)}, f32[120,128]{1,0:T(8,128)S(1)}, u32[]{:S(2)}, u32[]{:S(2)}) collective-permute-start(f32[120,128]{1,0:T(8,128)S(1)} %get-tuple-element.50), channel_id=1, source_target_pairs={{0,4},{4,8},{8,12},{12,16},{16,20},{20,24},{24,28},{1,5},{5,9},{9,... | collective-permute-start | bytes 184328 | tf_op jit(solution)/shard_map/ppermute | solution.py:427
  8.2 12.9 %collective-permute-start.1 = (f32[120,128]{1,0:T(8,128)S(1)}, f32[120,128]{1,0:T(8,128)S(1)}, u32[]{:S(2)}, u32[]{:S(2)}) collective-permute-start(f32[120,128]{1,0:T(8,128)S(1)} %get-tuple-element.51), channel_id=1, source_target_pairs={{4,0},{8,4},{12,8},{16,12},{20,16},{24,20},{28,24},{5,1},{9,5},{13... | collective-permute-start | bytes 184328 | tf_op jit(solution)/shard_map/ppermute | solution.py:427
  11.9 6.8 %collective-permute-start.2 = (f32[72,128]{1,0:T(8,128)S(1)}, f32[72,128]{1,0:T(8,128)S(1)}, u32[]{:S(2)}, u32[]{:S(2)}) collective-permute-start(f32[72,128]{1,0:T(8,128)S(1)} %get-tuple-element.52), channel_id=1, source_target_pairs={{0,1},{1,2},{2,3},{4,5},{5,6},{6,7},{8,9},{9,10},{10,11},{12,13},{... | collective-permute-start | bytes 110600 | tf_op jit(solution)/shard_map/ppermute | solution.py:427
  15.3 5.9 %collective-permute-start.3 = (f32[72,128]{1,0:T(8,128)S(1)}, f32[72,128]{1,0:T(8,128)S(1)}, u32[]{:S(2)}, u32[]{:S(2)}) collective-permute-start(f32[72,128]{1,0:T(8,128)S(1)} %get-tuple-element.53), channel_id=1, source_target_pairs={{1,0},{2,1},{3,2},{5,4},{6,5},{7,6},{9,8},{10,9},{11,10},{13,12},{... | collective-permute-start | bytes 110600 | tf_op jit(solution)/shard_map/ppermute | solution.py:427
  26.5 15.7 %collective-permute-start.4 = (f32[120,128]{1,0:T(8,128)S(1)}, f32[120,128]{1,0:T(8,128)S(1)}, u32[]{:S(2)}, u32[]{:S(2)}) collective-permute-start(f32[120,128]{1,0:T(8,128)S(1)} %get-tuple-element.66), channel_id=1, source_target_pairs={{0,4},{4,8},{8,12},{12,16},{16,20},{20,24},{24,28},{1,5},{5,9},{9,... | collective-permute-start | bytes 184328 | tf_op jit(solution)/shard_map/ppermute | solution.py:427
  28.4 13.8 %collective-permute-start.5 = (f32[120,128]{1,0:T(8,128)S(1)}, f32[120,128]{1,0:T(8,128)S(1)}, u32[]{:S(2)}, u32[]{:S(2)}) collective-permute-start(f32[120,128]{1,0:T(8,128)S(1)} %get-tuple-element.67), channel_id=1, source_target_pairs={{4,0},{8,4},{12,8},{16,12},{20,16},{24,20},{28,24},{5,1},{9,5},{13... | collective-permute-start | bytes 184328 | tf_op jit(solution)/shard_map/ppermute | solution.py:427
  32.1 7.2 %collective-permute-start.6 = (f32[72,128]{1,0:T(8,128)S(1)}, f32[72,128]{1,0:T(8,128)S(1)}, u32[]{:S(2)}, u32[]{:S(2)}) collective-permute-start(f32[72,128]{1,0:T(8,128)S(1)} %get-tuple-element.68), channel_id=1, source_target_pairs={{0,1},{1,2},{2,3},{4,5},{5,6},{6,7},{8,9},{9,10},{10,11},{12,13},{... | collective-permute-start | bytes 110600 | tf_op jit(solution)/shard_map/ppermute | solution.py:427
  36.4 5.9 %collective-permute-start.7 = (f32[72,128]{1,0:T(8,128)S(1)}, f32[72,128]{1,0:T(8,128)S(1)}, u32[]{:S(2)}, u32[]{:S(2)}) collective-permute-start(f32[72,128]{1,0:T(8,128)S(1)} %get-tuple-element.69), channel_id=1, source_target_pairs={{1,0},{2,1},{3,2},{5,4},{6,5},{7,6},{9,8},{10,9},{11,10},{13,12},{... | collective-permute-start | bytes 110600 | tf_op jit(solution)/shard_map/ppermute | solution.py:427

commit v3 on v2

--- a/solution.py
+++ b/solution.py
@@ -49,24 +49,25 @@
     return jnp.where(number + first == index_row, 1.0, 0.0).astype(BF16)
 
 
-def fold_depth(basis):
-    return -(-3 * basis // 64) * 64
+def fold_step(basis):
+    return -(-basis // 16) * 16
 
 
 def fold_rows(value):
     basis, lanes = value.shape
-    high = value.astype(BF16).astype(F32)
-    rest = jnp.zeros((fold_depth(basis) - 3 * basis, lanes), F32)
-    return jnp.concatenate([high, high, value - high, rest], axis=0).astype(BF16)
+    rest = jnp.zeros((fold_step(basis) - basis, lanes), F32)
+    value = jnp.concatenate([value, rest], axis=0)
+    high, low = halves(value)
+    return jnp.concatenate([high, high, low], axis=0)
 
 
 def fold_columns(matrix):
     basis = matrix.shape[1]
-    depth = fold_depth(basis)
+    step = fold_step(basis)
     high, low = halves(matrix)
-    row, column = iota((basis, depth), 0), iota((basis, depth), 1)
-    outer = jnp.where((column == row) | (column == row + 2 * basis), 1.0, 0.0).astype(BF16)
-    inner = jnp.where(column == row + basis, 1.0, 0.0).astype(BF16)
+    row, column = iota((basis, 3 * step), 0), iota((basis, 3 * step), 1)
+    outer = jnp.where((column == row) | (column == row + 2 * step), 1.0, 0.0).astype(BF16)
+    inner = jnp.where(column == row + step, 1.0, 0.0).astype(BF16)
     return (dot(high, outer) + dot(low, inner)).astype(BF16)
 
 
@@ -81,22 +82,26 @@
         for q in range(quants):
             for d in range(3):
                 block = stiffened[d * basis:(d + 1) * basis, q * lanes:(q + 1) * lanes]
+                block = block.reshape(basis // 8, 8, lanes)
                 for i in range(GROUP):
-                    term = block * jac[q, start + i, d:d + 1, :]
+                    term = block * jac[q, start + i, pl.ds(d, 8, stride=0), :]
                     totals[i] = term if totals[i] is None else totals[i] + term
-        take(start, totals)
+        take(start, [total.reshape(basis, lanes) for total in totals])
 
 
 def mix_faces(table, flux, side, quants, lanes, write):
     for f in range(4):
         blocks = [
-            table[q * ROWS:(q + 1) * ROWS, f * lanes:(f + 1) * lanes] for q in range(quants)
+            table[q * ROWS:(q + 1) * ROWS, f * lanes:(f + 1) * lanes].reshape(
+                ROWS // 8, 8, lanes
+            )
+            for q in range(quants)
         ]
         for p in range(quants):
-            total = blocks[0] * flux[side, 0, p, f:f + 1, :]
+            total = blocks[0] * flux[side, 0, p, pl.ds(f, 8, stride=0), :]
             for q in range(1, quants):
-                total = total + blocks[q] * flux[side, q, p, f:f + 1, :]
-            write(f, p, total)
+                total = total + blocks[q] * flux[side, q, p, pl.ds(f, 8, stride=0), :]
+            write(f, p, total.reshape(ROWS, lanes))
 
 
 def fill_projector(projector, padded):
@@ -135,6 +140,10 @@
                 table[q * ROWS:(q + 1) * ROWS, f * lanes:(f + 1) * lanes] = flat[
                     f * ROWS:(f + 1) * ROWS, (q - start) * lanes:(q - start + 1) * lanes
                 ]
+
+
+def even_spot():
+    return [lax.rem(lax.axis_index(axis), 2) == 0 for axis in ("dom", "sub")]
 
 
 def pick_sends(table, send_row, outs, lanes):
@@ -151,6 +160,13 @@
         jnp.where(lane < SLOTS_DOM, turned, low),
         jnp.where(left, spread, moved),
         jnp.where(left, moved, spread),
+    ]
+    even_dom, even_sub = even_spot()
+    pieces = [
+        jnp.where(even_dom, pieces[1], pieces[0]),
+        jnp.where(even_dom, pieces[0], pieces[1]),
+        jnp.where(even_sub, pieces[3], pieces[2]),
+        jnp.where(even_sub, pieces[2], pieces[3]),
     ]
     index = jnp.concatenate([piece[0:1] for piece in pieces], axis=1)
     chosen = one_hot(index, 0, faces)
@@ -194,7 +210,13 @@
         [spread_received(item[...], groups, lanes) for item, groups in zip(arrived, PACKING)],
         axis=1,
     )
-    starts = (faces, faces + SLOTS_DOM, faces + 2 * SLOTS_DOM, faces + 2 * SLOTS_DOM + SLOTS_SUB)
+    even_dom, even_sub = even_spot()
+    starts = (
+        jnp.where(even_dom, faces + SLOTS_DOM, faces),
+        jnp.where(even_dom, faces, faces + SLOTS_DOM),
+        faces + 2 * SLOTS_DOM + jnp.where(even_sub, SLOTS_SUB, 0),
+        faces + 2 * SLOTS_DOM + jnp.where(even_sub, 0, SLOTS_SUB),
+    )
     widths = (SLOTS_DOM, SLOTS_DOM, SLOTS_SUB, SLOTS_SUB)
     chosen = jnp.concatenate(
         [
@@ -323,14 +345,14 @@
 
 
 def third_kernel(
-    state, first, second, part, picked_local, from_lower, from_upper, from_left, from_right,
+    state, first, second, part, picked_local, dom_even, dom_odd, sub_even, sub_odd,
     jac, stiff_fold, padded, flux, slot, orient, cluster, lifting, send_row,
-    middle, integral, picked, table, to_lower, to_upper, to_left, to_right,
+    middle, integral, picked, table, send_dom_even, send_dom_odd, send_sub_even, send_sub_odd,
     stiffened, solved,
 ):
     quants, basis, lanes = state.shape
     picked[...] = picked_local[...] + pick_received(
-        (from_lower, from_upper, from_left, from_right), slot, 4 * lanes, lanes
+        (dom_even, dom_odd, sub_even, sub_odd), slot, 4 * lanes, lanes
     )
     near = near_lift(picked, flux, orient, lifting[...], solved, quants, lanes)
     fine = cluster[...] == 0
@@ -347,7 +369,9 @@
     )
     for q in range(quants):
         integral[q] = jnp.where(fine, integral[q], first[q] + second[q])
-    pick_sends(table, send_row, (to_lower, to_upper, to_left, to_right), lanes)
+    pick_sends(
+        table, send_row, (send_dom_even, send_dom_odd, send_sub_even, send_sub_odd), lanes
+    )
 
 
 def fourth_kernel(
@@ -374,14 +398,14 @@
 
 
 def fifth_kernel(
-    part, picked_local, from_lower, from_upper, from_left, from_right, flux, slot, orient, lifting,
+    part, picked_local, dom_even, dom_odd, sub_even, sub_odd, flux, slot, orient, lifting,
     yield_stress,
     updated,
     solved, picked,
 ):
     quants, basis, lanes = part.shape
     picked[...] = picked_local[...] + pick_received(
-        (from_lower, from_upper, from_left, from_right), slot, 4 * lanes, lanes
+        (dom_even, dom_odd, sub_even, sub_odd), slot, 4 * lanes, lanes
     )
     near = near_lift(picked, flux, orient, lifting[...], solved, quants, lanes)
     stepped = [part[q] - near[:, q * lanes:(q + 1) * lanes] for q in range(quants)]
@@ -419,19 +443,18 @@
 
 
 def exchange(sends):
-    to_lower, to_upper, to_left, to_right = sends
-
-    def shift(value, axis, step):
+    def swap(value, axis, first):
         size = lax.axis_size(axis)
-        pairs = [(i, i + step) for i in range(size) if 0 <= i + step < size]
-        return lax.ppermute(value, axis, pairs)
-
-    return (
-        shift(to_upper, "dom", 1),
-        shift(to_lower, "dom", -1),
-        shift(to_right, "sub", 1),
-        shift(to_left, "sub", -1),
-    )
+        lower = range(first, size - 1, 2)
+        return lax.ppermute(
+            value, axis, [(i, i + 1) for i in lower] + [(i + 1, i) for i in lower]
+        )
+
+    dom_odd = swap(sends[1], "dom", 1)
+    sub_odd = swap(sends[3], "sub", 1)
+    sub_even = swap(sends[2], "sub", 0)
+    dom_even = swap(sends[0], "dom", 0)
+    return dom_even, dom_odd, sub_even, sub_odd
 
 
 def on_device(
@@ -467,9 +490,8 @@
     field = (quants, basis, lanes)
     table = (quants * ROWS, 4 * lanes)
     messages = [(groups[0][1] * ROWS, lanes) for groups in PACKING]
-    depth = fold_depth(basis)
     flat = quants * lanes
-    fold = (3 * basis, depth)
+    fold = (3 * basis, 3 * fold_step(basis))
     stiffened = pltpu.VMEM((3 * basis, flat), F32)
     two_stiffened = pltpu.VMEM((2, 3 * basis, flat), F32)
     own_solved = pltpu.VMEM((4 * ROWS, flat), F32)

time: 44.6 us -> 34.8 us (0.78)
  the two profiles are of different devices: /device:TPU:8 before, /device:TPU:21 now
where the time goes in v3:
time: 34.8 us; the launch traced here: 34.6 us
  Pallas kernels  17.3 us (50%)
  starting transfers between devices  12.8 us (37%)
  waiting for transfers between devices  4.46 us (13%)
    pallas_call x5, Pallas kernels, run(): pl.pallas_call(body, out_shape=[out if isinstance(out, jax.ShapeDtypeStru...  17.3 us
    ppermute x8, starting transfers between devices, swap(): lax.ppermute(value, axis, [(i, i + 1) for i in lower] + [(i + 1, i) for i...  12.8 us
    ppermute x8, waiting for transfers between devices, swap(): lax.ppermute(value, axis, [(i, i + 1) for i in lower] + [(i + 1, i) for i...  4.46 us
  transfers between devices with their start and end apart: 8, of which 2 were waited for; matrix products, arithmetic and copies ran while one was open for 0% of the time, Pallas kernels for 11%

profile of v3, /device:TPU:21, one launch (start us, length us, event | category | flops | bytes accessed | tf_op | source)
XLA Modules:
  0.0 34.6 jit_solution(6268008952577564061)
XLA Ops:
  0.0 6.3 %first_kernel.1 = (f32[9,56,128]{2,1,0:T(8,128)S(1)}, f32[3,56,56]{2,1,0:T(8,128)S(1)}, f32[21,4,56]{2,1,0:T(4,128)}, f32[9,9,3,128]{3,2,1,0:T(4,128)S(1)}, s32[...) custom-call(f32[9,56,128]{2,1,0:T(8,128)} %bitcast.9, ...), custom_call_target="tpu_custom_call" | custom-call | tf_op jit(solution)/shard_map/first_kernel/pallas_call | solution.py:431
  6.3 0.7 %collective-permute-start = (f32[120,128]{1,0:T(8,128)S(1)}, f32[120,128]{1,0:T(8,128)S(1)}, u32[]{:S(2)}, u32[]{:S(2)}) collective-permute-start(f32[120,128]{1,0:T(8,128)S(1)} %get-tuple-element.50), channel_id=1, source_target_pairs={{0,4},{8,12},{16,20},{24,28},{4,0},{12,8},{20,16},{28,24},{1,5},{9... | collective-permute-start | bytes 184328 | tf_op jit(solution)/shard_map/ppermute | solution.py:449
  7.0 3.1 %collective-permute-start.1 = (f32[120,128]{1,0:T(8,128)S(1)}, f32[120,128]{1,0:T(8,128)S(1)}, u32[]{:S(2)}, u32[]{:S(2)}) collective-permute-start(f32[120,128]{1,0:T(8,128)S(1)} %get-tuple-element.51), channel_id=1, source_target_pairs={{4,8},{12,16},{20,24},{8,4},{16,12},{24,20},{5,9},{13,17},{21,25},... | collective-permute-start | bytes 184328 | tf_op jit(solution)/shard_map/ppermute | solution.py:449
  10.1 1.3 %collective-permute-start.2 = (f32[72,128]{1,0:T(8,128)S(1)}, f32[72,128]{1,0:T(8,128)S(1)}, u32[]{:S(2)}, u32[]{:S(2)}) collective-permute-start(f32[72,128]{1,0:T(8,128)S(1)} %get-tuple-element.52), channel_id=1, source_target_pairs={{0,1},{2,3},{1,0},{3,2},{4,5},{6,7},{5,4},{7,6},{8,9},{10,11},{9,8... | collective-permute-start | bytes 110600 | tf_op jit(solution)/shard_map/ppermute | solution.py:449
  11.4 2.1 %collective-permute-start.3 = (f32[72,128]{1,0:T(8,128)S(1)}, f32[72,128]{1,0:T(8,128)S(1)}, u32[]{:S(2)}, u32[]{:S(2)}) collective-permute-start(f32[72,128]{1,0:T(8,128)S(1)} %get-tuple-element.53), channel_id=1, source_target_pairs={{1,2},{2,1},{5,6},{6,5},{9,10},{10,9},{13,14},{14,13},{17,18},{18,... | collective-permute-start | bytes 110600 | tf_op jit(solution)/shard_map/ppermute | solution.py:449
  13.5 2.1 %second_kernel.1 = (f32[9,56,128]{2,1,0:T(8,128)S(1)}, f32[216,512]{1,0:T(8,128)S(1)}, f32[56,288]{1,0:T(8,128)S(1)}, f32[168,192]{1,0:T(8,128)S(1)}) custom-call(f32[9,56,128]{2,1,0:T(8,128)S(1)} %get-tuple-element.38.state, f32[9,56,128]{2,1,0:T(8,128)S(1)} %get-tuple-element.39.first, f32[216,512]{1,0:T(8,128)S(1)} %get-tuple-element.41.table.table_one, ...), custom_call_target="tpu_custom_call" | custom-call | tf_op jit(solution)/shard_map/second_kernel/pallas_call | solution.py:431
  15.6 0.0 collective-permute-done.2.sub_even
  15.7 1.9 %collective-permute-done.3.sub_odd = f32[72,128]{1,0:T(8,128)S(1)} collective-permute-done((f32[72,128]{1,0:T(8,128)S(1)}, f32[72,128]{1,0:T(8,128)S(1)}, u32[]{:S(2)}, u32[]{:S(2)}) %collective-permute-start.3) | collective-permute-done | bytes 36896 | tf_op jit(solution)/shard_map/ppermute | solution.py:449
  17.6 0.0 collective-permute-done.dom_even
  17.6 0.0 collective-permute-done.1.dom_odd
  17.6 5.3 %third_kernel.1 = (f32[9,56,128]{2,1,0:T(8,128)S(1)}, f32[9,56,128]{2,1,0:T(8,128)S(1)}, f32[216,512]{1,0:T(8,128)S(1)}, f32[216,512]{1,0:T(8,128)S(1)}, f32[120...) custom-call(f32[9,56,128]{2,1,0:T(8,128)S(1)} %get-tuple-element.38.state, ...), custom_call_target="tpu_custom_call" | custom-call | tf_op jit(solution)/shard_map/third_kernel/pallas_call | solution.py:431
  22.9 0.6 %collective-permute-start.4 = (f32[120,128]{1,0:T(8,128)S(1)}, f32[120,128]{1,0:T(8,128)S(1)}, u32[]{:S(2)}, u32[]{:S(2)}) collective-permute-start(f32[120,128]{1,0:T(8,128)S(1)} %get-tuple-element.66), channel_id=1, source_target_pairs={{0,4},{8,12},{16,20},{24,28},{4,0},{12,8},{20,16},{28,24},{1,5},{9... | collective-permute-start | bytes 184328 | tf_op jit(solution)/shard_map/ppermute | solution.py:449
  23.5 2.8 %collective-permute-start.5 = (f32[120,128]{1,0:T(8,128)S(1)}, f32[120,128]{1,0:T(8,128)S(1)}, u32[]{:S(2)}, u32[]{:S(2)}) collective-permute-start(f32[120,128]{1,0:T(8,128)S(1)} %get-tuple-element.67), channel_id=1, source_target_pairs={{4,8},{12,16},{20,24},{8,4},{16,12},{24,20},{5,9},{13,17},{21,25},... | collective-permute-start | bytes 184328 | tf_op jit(solution)/shard_map/ppermute | solution.py:449
  26.3 0.1 collective-permute-start.6
  26.4 2.1 %collective-permute-start.7 = (f32[72,128]{1,0:T(8,128)S(1)}, f32[72,128]{1,0:T(8,128)S(1)}, u32[]{:S(2)}, u32[]{:S(2)}) collective-permute-start(f32[72,128]{1,0:T(8,128)S(1)} %get-tuple-element.69), channel_id=1, source_target_pairs={{1,2},{2,1},{5,6},{6,5},{9,10},{10,9},{13,14},{14,13},{17,18},{18,... | collective-permute-start | bytes 110600 | tf_op jit(solution)/shard_map/ppermute | solution.py:449
  28.5 1.5 %fourth_kernel.1 = (f32[9,56,128]{2,1,0:T(8,128)S(1)}, f32[216,512]{1,0:T(8,128)S(1)}) custom-call(f32[9,56,128]{2,1,0:T(8,128)S(1)} %get-tuple-element.59.middle, f32[9,56,128]{2,1,0:T(8,128)S(1)} %get-tuple-element.60.integral, f32[216,512]{1,0:T(8,128)S(1)} %get-tuple-element.41.table.table_one, f32[216,512]{1,0:T(8,128)S(1)} %get-tuple-element.61.table_two, ...), custom_call_target="tpu_custom_call" | custom-call | tf_op jit(solution)/shard_map/fourth_kernel/pallas_call | solution.py:431
  30.0 0.0 collective-permute-done.6.sub_even
  30.0 2.5 %collective-permute-done.7.sub_odd = f32[72,128]{1,0:T(8,128)S(1)} collective-permute-done((f32[72,128]{1,0:T(8,128)S(1)}, f32[72,128]{1,0:T(8,128)S(1)}, u32[]{:S(2)}, u32[]{:S(2)}) %collective-permute-start.7) | collective-permute-done | bytes 36896 | tf_op jit(solution)/shard_map/ppermute | solution.py:449
  32.6 0.0 collective-permute-done.4.dom_even
  32.6 0.0 collective-permute-done.5.dom_odd
  32.6 2.0 %fifth_kernel.1 = f32[9,56,128]{2,1,0:T(8,128)} custom-call(f32[9,56,128]{2,1,0:T(8,128)S(1)} %get-tuple-element.64.part, f32[216,512]{1,0:T(8,128)S(1)} %get-tuple-element.65.picked_local, f32[120,128]{1,0:T(8,128)S(1)} %collective-permute-done.4.dom_even, f32[120,128]{1,0:T(8,128)S(1)} %collective-permute-done.5.dom_odd, ...), custom_call_target="tpu_custom_call" | custom-call | tf_op jit(solution)/shard_map/fifth_kernel/pallas_call | solution.py:431
Async XLA Ops:
  6.3 11.3 %collective-permute-start = (f32[120,128]{1,0:T(8,128)S(1)}, f32[120,128]{1,0:T(8,128)S(1)}, u32[]{:S(2)}, u32[]{:S(2)}) collective-permute-start(f32[120,128]{1,0:T(8,128)S(1)} %get-tuple-element.50), channel_id=1, source_target_pairs={{0,4},{8,12},{16,20},{24,28},{4,0},{12,8},{20,16},{28,24},{1,5},{9... | collective-permute-start | bytes 184328 | tf_op jit(solution)/shard_map/ppermute | solution.py:449
  7.0 10.6 %collective-permute-start.1 = (f32[120,128]{1,0:T(8,128)S(1)}, f32[120,128]{1,0:T(8,128)S(1)}, u32[]{:S(2)}, u32[]{:S(2)}) collective-permute-start(f32[120,128]{1,0:T(8,128)S(1)} %get-tuple-element.51), channel_id=1, source_target_pairs={{4,8},{12,16},{20,24},{8,4},{16,12},{24,20},{5,9},{13,17},{21,25},... | collective-permute-start | bytes 184328 | tf_op jit(solution)/shard_map/ppermute | solution.py:449
  10.1 5.5 %collective-permute-start.2 = (f32[72,128]{1,0:T(8,128)S(1)}, f32[72,128]{1,0:T(8,128)S(1)}, u32[]{:S(2)}, u32[]{:S(2)}) collective-permute-start(f32[72,128]{1,0:T(8,128)S(1)} %get-tuple-element.52), channel_id=1, source_target_pairs={{0,1},{2,3},{1,0},{3,2},{4,5},{6,7},{5,4},{7,6},{8,9},{10,11},{9,8... | collective-permute-start | bytes 110600 | tf_op jit(solution)/shard_map/ppermute | solution.py:449
  11.4 6.2 %collective-permute-start.3 = (f32[72,128]{1,0:T(8,128)S(1)}, f32[72,128]{1,0:T(8,128)S(1)}, u32[]{:S(2)}, u32[]{:S(2)}) collective-permute-start(f32[72,128]{1,0:T(8,128)S(1)} %get-tuple-element.53), channel_id=1, source_target_pairs={{1,2},{2,1},{5,6},{6,5},{9,10},{10,9},{13,14},{14,13},{17,18},{18,... | collective-permute-start | bytes 110600 | tf_op jit(solution)/shard_map/ppermute | solution.py:449
  22.9 9.6 %collective-permute-start.4 = (f32[120,128]{1,0:T(8,128)S(1)}, f32[120,128]{1,0:T(8,128)S(1)}, u32[]{:S(2)}, u32[]{:S(2)}) collective-permute-start(f32[120,128]{1,0:T(8,128)S(1)} %get-tuple-element.66), channel_id=1, source_target_pairs={{0,4},{8,12},{16,20},{24,28},{4,0},{12,8},{20,16},{28,24},{1,5},{9... | collective-permute-start | bytes 184328 | tf_op jit(solution)/shard_map/ppermute | solution.py:449
  23.5 9.1 %collective-permute-start.5 = (f32[120,128]{1,0:T(8,128)S(1)}, f32[120,128]{1,0:T(8,128)S(1)}, u32[]{:S(2)}, u32[]{:S(2)}) collective-permute-start(f32[120,128]{1,0:T(8,128)S(1)} %get-tuple-element.67), channel_id=1, source_target_pairs={{4,8},{12,16},{20,24},{8,4},{16,12},{24,20},{5,9},{13,17},{21,25},... | collective-permute-start | bytes 184328 | tf_op jit(solution)/shard_map/ppermute | solution.py:449
  26.3 3.7 %collective-permute-start.6 = (f32[72,128]{1,0:T(8,128)S(1)}, f32[72,128]{1,0:T(8,128)S(1)}, u32[]{:S(2)}, u32[]{:S(2)}) collective-permute-start(f32[72,128]{1,0:T(8,128)S(1)} %get-tuple-element.68), channel_id=1, source_target_pairs={{0,1},{2,3},{1,0},{3,2},{4,5},{6,7},{5,4},{7,6},{8,9},{10,11},{9,8... | collective-permute-start | bytes 110600 | tf_op jit(solution)/shard_map/ppermute | solution.py:449
  26.4 6.2 %collective-permute-start.7 = (f32[72,128]{1,0:T(8,128)S(1)}, f32[72,128]{1,0:T(8,128)S(1)}, u32[]{:S(2)}, u32[]{:S(2)}) collective-permute-start(f32[72,128]{1,0:T(8,128)S(1)} %get-tuple-element.69), channel_id=1, source_target_pairs={{1,2},{2,1},{5,6},{6,5},{9,10},{10,9},{13,14},{14,13},{17,18},{18,... | collective-permute-start | bytes 110600 | tf_op jit(solution)/shard_map/ppermute | solution.py:449
